TPU v7x, 32 devices: a whole 2x2x4 slice. The times are simulated.
32 devices in a mesh: lon: 8 (over z, core), lat: 4 (over y, x).
Axes of the slice: x: 2, y: 2, z: 4, core: 2. Of those that a mesh axis runs over, the one named last changes fastest.
Arguments:
- ensemble_prediction: bfloat16 [408, 256, 2048], P(None, 'lat', 'lon'), may hold values from -6 to 6
- mapping_matrix: bfloat16 [96, 408], replicated, may hold values from -0.3125 to 0.3125
- mapping_offset: float32 [96], replicated, may hold values from -3 to 3
- gauge_measured_records: bfloat16 [131072, 256], P(('lon', 'lat')), may hold values from -6 to 6
- gauge_scatter_matrix: bfloat16 [256, 96], replicated, may hold values from -0.375 to 0.375
- gauge_scatter_offset: float32 [96], replicated, may hold values from -3 to 3
- gauge_block_number: int32 [131072, 1], P(('lon', 'lat')), may hold values from 0 to 31; in each aligned block of 4096 rows (0 to 4095, 4096 to 8191, ...) at most 256 rows name the same one
- gauge_point_position: int32 [131072], P(('lon', 'lat')), may hold values from 0 to 16383
- initial_filter_matrix: bfloat16 [96, 96, 3, 3], replicated, may hold values from -0.21875 to 0.21875
- initial_filter_offset: float32 [96], replicated, may hold values from -3 to 3
- latter_filter_matrix: bfloat16 [96, 96, 3, 3], replicated, may hold values from -0.21875 to 0.21875
- latter_filter_offset: float32 [96], replicated, may hold values from -3 to 3
Outputs:
- corrected: bfloat16 [96, 256, 2048], P(None, 'lat', 'lon')
- station_values: bfloat16 [131072, 96], P(('lon', 'lat'))
Inputs may be any that keep to these rules, and one draw needn't show every extreme that they name: `gauge_block_number`: among the 4096 rows of one device, at most 256 name the same tile, a bound that some block reaches.
All inputs are finite; a program needn't handle non-finite values.
Results may differ from a plain program's by a relative error of at most 0.01.
Values may be sent and summed in bfloat16 or wider, within the bound.
A program may use at most 192 MiB of HBM per device.

v0:
```python
import jax
import jax.numpy as jnp
from jax import lax
from jax.sharding import PartitionSpec as P


def extended(block, sides, width, periodic):
    for axis, dim in sides:
        count = lax.axis_size(axis)
        forward = [(i, i + 1) for i in range(count - 1)]
        if periodic:
            forward.append((count - 1, 0))
        backward = [(target, source) for source, target in forward]
        low = lax.ppermute(
            lax.slice_in_dim(block, block.shape[dim] - width, None, axis=dim), axis, forward
        )
        high = lax.ppermute(lax.slice_in_dim(block, 0, width, axis=dim), axis, backward)
        block = jnp.concatenate([low, block, high], axis=dim)
    return block


def conv_valid(field, kernel):
    result = lax.conv_general_dilated(
        field[None],
        kernel,
        (1, 1),
        "VALID",
        dimension_numbers=("NCHW", "OIHW", "NCHW"),
        preferred_element_type=jnp.float32,
    )
    return result[0]


def on_device(
    ensemble_prediction,
    mapping_matrix,
    mapping_offset,
    gauge_measured_records,
    gauge_scatter_matrix,
    gauge_scatter_offset,
    gauge_block_number,
    gauge_point_position,
    initial_filter_matrix,
    initial_filter_offset,
    latter_filter_matrix,
    latter_filter_offset,
):
    feature_depth_total, north_south_total, east_west_total = ensemble_prediction.shape
    features = mapping_matrix.shape[0]
    mesh_point_total = north_south_total * east_west_total
    lon_size = lax.axis_size("lon")
    lat_size = lax.axis_size("lat")
    devices = lon_size * lat_size
    held_rows = gauge_measured_records.shape[0]
    capacity = 2 * held_rows // devices
    slot_total = devices * capacity
    target_tile = gauge_block_number[:, 0]
    one_hot = (target_tile[:, None] == jnp.arange(devices, dtype=jnp.int32)[None, :]).astype(
        jnp.int32
    )
    earlier = jnp.cumsum(one_hot, axis=0) - one_hot
    slot_index = jnp.sum(earlier * one_hot, axis=1)
    position = target_tile * capacity + slot_index
    local_embedded = (
        jnp.dot(gauge_measured_records, gauge_scatter_matrix, preferred_element_type=jnp.float32)
        + gauge_scatter_offset[None, :]
    ).astype(jnp.bfloat16)
    payload = jnp.zeros((slot_total, features), jnp.bfloat16).at[position].set(local_embedded)
    cell_slots = jnp.full((slot_total,), -1, jnp.int32).at[position].set(gauge_point_position)
    arrived, arrived_cells = (
        lax.all_to_all(
            payload.reshape(devices, capacity, payload.shape[1]),
            ("lon", "lat"),
            split_axis=0,
            concat_axis=0,
            tiled=True,
        ),
        lax.all_to_all(
            cell_slots.reshape(devices, capacity),
            ("lon", "lat"),
            split_axis=0,
            concat_axis=0,
            tiled=True,
        ),
    )
    arrived = arrived.reshape(slot_total, payload.shape[1])
    arrived_cells = arrived_cells.reshape(slot_total)
    mapped_features = (
        jnp.dot(
            mapping_matrix,
            ensemble_prediction.reshape(feature_depth_total, mesh_point_total),
            preferred_element_type=jnp.float32,
        )
        + mapping_offset[:, None]
    )
    scatter_cell = jnp.where(arrived_cells >= 0, arrived_cells, mesh_point_total)
    merged_sum = mapped_features.at[:, scatter_cell].add(arrived.astype(jnp.float32).T, mode="drop")
    merged = merged_sum.astype(jnp.bfloat16).reshape(features, north_south_total, east_west_total)

    def extend(field):
        rimmed = extended(field, (("lon", 2),), 1, True)
        return extended(rimmed, (("lat", 1),), 1, False)

    hidden = jax.nn.gelu(
        conv_valid(extend(merged), initial_filter_matrix) + initial_filter_offset[:, None, None]
    ).astype(jnp.bfloat16)
    second = conv_valid(extend(hidden), latter_filter_matrix)
    corrected = (merged.astype(jnp.float32) + second + latter_filter_offset[:, None, None]).astype(
        jnp.bfloat16
    )
    read_cell = jnp.clip(arrived_cells, 0, mesh_point_total - 1)
    picked = corrected.reshape(features, mesh_point_total)[:, read_cell].T
    returned = lax.all_to_all(
        picked.reshape(devices, capacity, features),
        ("lon", "lat"),
        split_axis=0,
        concat_axis=0,
        tiled=True,
    )
    station_values = returned.reshape(slot_total, features)[position]
    return (corrected, station_values)


def solution(mesh):
    placed = (
        P(None, "lat", "lon"),
        P(),
        P(),
        P(("lon", "lat"), None),
        P(),
        P(),
        P(("lon", "lat"), None),
        P(("lon", "lat")),
        P(),
        P(),
        P(),
        P(),
    )
    return jax.shard_map(
        on_device,
        mesh=mesh,
        in_specs=placed,
        out_specs=(P(None, "lat", "lon"), P(("lon", "lat"), None)),
        check_vma=False,
    )
```

profile of v0, /device:TPU:0, one launch (start us, length us, event | category | flops | bytes accessed | tf_op | source)
XLA Modules:
  0.0 337.8 jit_solution(3211927603797979571)
XLA Ops:
  1.6 9.2 %reduce-window.6 = s32[32,32,128]{2,1,0:T(8,128)S(1)} reduce-window(s32[32,32,128]{2,1,0:T(8,128)S(1)} %fusion.41, s32[]{:T(128)} %constant.13.clone.1), window={size=1x1x128 pad=0_0x0_0x127_0}, to_apply=%region_0.0 | reduce-window | flops 16646144 | bytes 1048580 | tf_op jit(solution)/shard_map/reduce-window
  13.9 16.3 %scatter_custom_fusion = s32[8192]{0:T(1024)} fusion(s32[4096]{0:T(1024)S(1)} %bitcast.106, s32[4096]{0:T(1024)} %param.19, s32[]{:T(128)} %constant.11.clone.1), kind=kCustom, calls=%fused_computation.66 | custom fusion | bytes 33280 | tf_op jit(solution)/shard_map/scatter | solution.py:69
  30.2 7.3 %all-to-all-start = ((s32[32,1,256]{2,1,0:T(1,128)}), s32[32,1,256]{2,1,0:T(1,128)S(1)}, u32[]{:S(2)}, u32[]{:S(2)}) async-start(s32[32,1,256]{2,1,0:T(1,128)} %bitcast.5), calls=%async_computation | async-start | bytes 65536 | tf_op jit(solution)/shard_map/all_to_all | solution.py:78
  37.5 1.6 fusion.29
  39.1 1.3 copy.51
  40.4 11.9 %scatter_custom_fusion.1 = bf16[8192,96]{1,0:T(8,128)(2,1)S(1)} fusion(s32[4096]{0:T(1024)S(1)} %bitcast.107, bf16[4096,96]{1,0:T(8,128)(2,1)} %copy.51, bf16[]{:T(256)} %constant.4.clone.1), kind=kCustom, calls=%fused_computation.47 | custom fusion | bytes 1573376 | tf_op jit(solution)/shard_map/scatter | solution.py:68
  52.2 2.8 copy.52
  55.0 6.1 %all-to-all-start.1 = ((bf16[32,256,96]{1,2,0:T(8,128)(2,1)}), bf16[32,256,96]{1,2,0:T(8,128)(2,1)S(1)}, u32[]{:S(2)}, u32[]{:S(2)}) async-start(bf16[32,256,96]{1,2,0:T(8,128)(2,1)} %copy.52), calls=%async_computation.1 | async-start | bytes 3145728 | tf_op jit(solution)/shard_map/all_to_all | solution.py:71
  61.1 12.7 %copy.73 = bf16[51,8,64,256]{3,1,2,0:T(8,128)(2,1)S(1)} copy(bf16[51,8,64,256]{3,2,1,0:T(8,128)(2,1)} %bitcast.95) | data formatting | bytes 26738688
  73.8 6.1 %convolution_add_fusion = f32[96,16384]{1,0:T(8,128)} fusion(bf16[96,408]{1,0:T(8,128)(2,1)S(1)} %copy-done.4, bf16[408,16384]{1,0:T(8,128)(2,1)S(1)} %bitcast.86, f32[96]{0:T(128)S(1)} %copy-done.6), kind=kOutput, calls=%fused_computation.5 | convolution fusion | flops 1285029888 | bytes 19739520 | tf_op jit(solution)/shard_map/dot_general | solution.py:89
  79.8 8.4 %copy.54 = f32[96,16384]{0,1:T(8,128)} copy(f32[96,16384]{1,0:T(8,128)} %convolution_add_fusion) | data formatting | bytes 12582912 | tf_op jit(solution)/shard_map/add | solution.py:89
  88.3 10.2 %all-to-all-done.1 = bf16[32,256,96]{1,2,0:T(8,128)(2,1)S(1)} async-done(((bf16[32,256,96]{1,2,0:T(8,128)(2,1)}), bf16[32,256,96]{1,2,0:T(8,128)(2,1)S(1)}, u32[]{:S(2)}, u32[]{:S(2)}) %all-to-all-start.1) | async-done | bytes 1572896 | tf_op jit(solution)/shard_map/all_to_all | solution.py:71
  98.5 2.9 copy.71
  101.4 46.4 %scatter_fusion = f32[96,16384]{0,1:T(8,128)} fusion(f32[96,16384]{0,1:T(8,128)} %copy.54, s32[8192]{0:T(1024)S(1)} %bitcast.101, f32[8192,96]{1,0:T(8,128)} %bitcast.94), kind=kCustom, calls=%fused_computation.4 | custom fusion | flops 786432 | bytes 9469952 | tf_op jit(solution)/shard_map/scatter-add | solution.py:97
  147.8 3.7 %convert_element_type.36 = bf16[96,16384]{0,1:T(8,128)(2,1)S(1)} convert(f32[96,16384]{0,1:T(8,128)} %scatter_fusion) | non-fusion elementwise | flops 1572864 | bytes 9437184 | tf_op jit(solution)/shard_map/convert_element_type | solution.py:98
  151.7 3.5 %collective-permute-start.1 = (bf16[96,64,1]{0,1,2:T(8,128)(2,1)S(1)}, bf16[96,64,1]{0,1,2:T(8,128)(2,1)S(1)}, u32[]{:S(2)}, u32[]{:S(2)}) collective-permute-start(bf16[96,64,1]{0,1,2:T(8,128)(2,1)S(1)} %copy.79), channel_id=1, source_target_pairs={{4,0},{8,4},{12,8},{16,12},{20,16},{24,20},{28,24},{0,28},{5,1},{9... | collective-permute-start | bytes 36872 | tf_op jit(solution)/shard_map/ppermute | solution.py:17
  155.2 1.4 collective-permute-done
  156.6 3.0 constant_dynamic-update-slice_fusion.1
  159.9 3.5 %collective-permute-start.2 = (bf16[96,1,258]{0,1,2:T(2,128)(2,1)S(1)}, bf16[96,1,258]{0,1,2:T(2,128)(2,1)S(1)}, u32[]{:S(2)}, u32[]{:S(2)}) collective-permute-start(bf16[96,1,258]{0,1,2:T(2,128)(2,1)S(1)} %get-tuple-element.12), channel_id=1, source_target_pairs={{0,1},{1,2},{2,3},{4,5},{5,6},{6,7},{8,9},{9,10},{10,11},{12,13},{... | collective-permute-start | bytes 148616 | tf_op jit(solution)/shard_map/ppermute | solution.py:14
  163.4 1.3 collective-permute-start.3
  164.7 1.2 collective-permute-done.2
  165.9 4.4 %collective-permute-done.3 = bf16[96,1,258]{0,1,2:T(2,128)(2,1)S(1)} collective-permute-done((bf16[96,1,258]{0,1,2:T(2,128)(2,1)S(1)}, bf16[96,1,258]{0,1,2:T(2,128)(2,1)S(1)}, u32[]{:S(2)}, u32[]{:S(2)}) %collective-permute-start.3) | collective-permute-done | bytes 49568 | tf_op jit(solution)/shard_map/ppermute | solution.py:17
  170.3 3.1 maximum_bitcast_fusion
  175.3 10.6 %broadcast_select_fusion.1 = f32[64,8,33,96]{3,1,2,0:T(8,128)S(1)} fusion(pred[8,33]{0,1:T(8,128)(4,1)S(1)} %copy-done.10, bf16[96,96,3,3]{1,0,3,2:T(8,128)(2,1)S(1)} %copy-done.8, bf16[96,66,1,7,2]{0,3,4,1,2:T(8,128)(2,1)S(1)} %slice.54, bf16[96,66,1,8,33]{0,3,4,1,2:T(8,128)(2,1)S(1)} %copy.61), kind=kOutput, calls=%fused_computation.44 | convolution fusion | flops 2815110144 | bytes 10177032 | tf_op jit(solution)/shard_map/conv_general_dilated | solution.py:23
  185.9 1.8 copy.62
  187.8 3.0 fusion.9
  190.9 3.5 %collective-permute-start.5 = (bf16[96,64,1]{0,1,2:T(8,128)(2,1)S(1)}, bf16[96,64,1]{0,1,2:T(8,128)(2,1)S(1)}, u32[]{:S(2)}, u32[]{:S(2)}) collective-permute-start(bf16[96,64,1]{0,1,2:T(8,128)(2,1)S(1)} %get-tuple-element.15), channel_id=1, source_target_pairs={{4,0},{8,4},{12,8},{16,12},{20,16},{24,20},{28,24},{0,28},{5,1},{9... | collective-permute-start | bytes 36872 | tf_op jit(solution)/shard_map/ppermute | solution.py:17
  194.4 1.4 collective-permute-done.4
  196.2 4.3 %collective-permute-start.6 = (bf16[96,1,258]{0,1,2:T(2,128)(2,1)S(1)}, bf16[96,1,258]{0,1,2:T(2,128)(2,1)S(1)}, u32[]{:S(2)}, u32[]{:S(2)}) collective-permute-start(bf16[96,1,258]{0,1,2:T(2,128)(2,1)S(1)} %get-tuple-element.10), channel_id=1, source_target_pairs={{0,1},{1,2},{2,3},{4,5},{5,6},{6,7},{8,9},{9,10},{10,11},{12,13},{... | collective-permute-start | bytes 148616 | tf_op jit(solution)/shard_map/ppermute | solution.py:14
  200.5 1.3 collective-permute-start.7
  201.8 1.2 collective-permute-done.6
  203.0 4.4 %collective-permute-done.7 = bf16[96,1,258]{0,1,2:T(2,128)(2,1)S(1)} collective-permute-done((bf16[96,1,258]{0,1,2:T(2,128)(2,1)S(1)}, bf16[96,1,258]{0,1,2:T(2,128)(2,1)S(1)}, u32[]{:S(2)}, u32[]{:S(2)}) %collective-permute-start.7) | collective-permute-done | bytes 49568 | tf_op jit(solution)/shard_map/ppermute | solution.py:17
  207.3 5.9 %maximum_bitcast_fusion.1 = bf16[96,66,1,258]{0,1,3,2:T(8,128)(2,1)S(1)} fusion(bf16[96,1,258]{0,1,2:T(2,128)(2,1)S(1)} %collective-permute-done.7, bf16[96,64,1]{0,1,2:T(8,128)(2,1)S(1)} %collective-permute-done.5, bf16[96,64,256]{0,1,2:T(8,128)(2,1)S(1)} %fusion.9, bf16[96,64,1]{0,1,2:T(8,128)(2,1)S(1)} %collective-permute-done.4, ...), kind=kLoop, calls=%fused_computation.29 | loop fusion | flops 16346880 | bytes 6538752 | tf_op jit(solution)/shard_map/broadcast_in_dim | solution.py:24
  215.1 10.6 %broadcast_select_fusion = f32[64,8,33,96]{3,1,2,0:T(8,128)S(1)} fusion(pred[8,33]{0,1:T(8,128)(4,1)S(1)} %copy-done.10, bf16[96,96,3,3]{1,0,3,2:T(8,128)(2,1)S(1)} %copy-done.9, bf16[96,66,1,7,2]{0,3,4,1,2:T(8,128)(2,1)S(1)} %slice.58, bf16[96,66,1,8,33]{0,3,4,1,2:T(8,128)(2,1)S(1)} %copy.64), kind=kOutput, calls=%fused_computation.43 | convolution fusion | flops 2815110144 | bytes 10177032 | tf_op jit(solution)/shard_map/conv_general_dilated | solution.py:23
  225.7 1.9 copy.65
  227.6 3.3 copy-done.2
  231.0 4.1 %slice_bitcast_fusion.1 = f32[1,96,64,256]{1,2,3,0:T(8,128)} fusion(f32[64,1,264,96]{3,0,2,1:T(8,128)S(1)} %bitcast.84), kind=kLoop, calls=%fused_computation.26 | loop fusion | bytes 12582912 | tf_op jit(solution)/shard_map/conv_general_dilated | solution.py:23
  235.1 11.7 %copy.66 = f32[1,96,64,256]{1,3,2,0:T(8,128)} copy(f32[1,96,64,256]{1,2,3,0:T(8,128)} %slice_bitcast_fusion.1) | data formatting | bytes 12582912 | tf_op jit(solution)/shard_map/conv_general_dilated | solution.py:23
  246.8 5.5 %fusion.14 = bf16[96,16384]{0,1:T(8,128)(2,1)} fusion(f32[1,96,64,256]{1,3,2,0:T(8,128)} %copy.66, f32[96]{0:T(128)S(1)} %copy-done.5, f32[96,16384]{0,1:T(8,128)S(1)} %bitcast.83), kind=kLoop, calls=%fused_computation.25 | loop fusion | flops 7864320 | bytes 15729024 | tf_op jit(solution)/shard_map/convert_element_type | solution.py:108
  252.3 24.6 %gather_fusion = bf16[8192,96]{1,0:T(8,128)(2,1)S(1)} fusion(bf16[96,16384]{0,1:T(8,128)(2,1)} %fusion.14, s32[8192]{0:T(1024)S(1)} %broadcast_clamp_fusion), kind=kCustom, calls=%fused_computation | custom fusion | bytes 3178496 | tf_op jit(solution)/shard_map/gather | solution.py:112
  276.9 2.8 copy.67
  279.7 3.5 %all-to-all-start.2 = ((bf16[32,256,96]{1,2,0:T(8,128)(2,1)}), bf16[32,256,96]{1,2,0:T(8,128)(2,1)S(1)}, u32[]{:S(2)}, u32[]{:S(2)}) async-start(bf16[32,256,96]{1,2,0:T(8,128)(2,1)} %copy.67), calls=%async_computation.2 | async-start | bytes 3145728 | tf_op jit(solution)/shard_map/all_to_all | solution.py:113
  283.2 7.7 %fusion.12 = bf16[96,64,256]{0,1,2:T(8,128)(2,1)} fusion(f32[64,1,264,96]{3,0,2,1:T(8,128)} %bitcast.85, f32[96]{0:T(128)S(1)} %copy-done.5, bf16[96,64,256]{0,2,1:T(8,128)(2,1)} %bitcast.90), kind=kLoop, calls=%fused_computation.22 | loop fusion | flops 6291456 | bytes 12583296 | tf_op jit(solution)/shard_map/convert_element_type | solution.py:108
  290.9 7.0 %copy.69 = bf16[96,64,256]{2,1,0:T(8,128)(2,1)} copy(bf16[96,64,256]{0,1,2:T(8,128)(2,1)} %fusion.12) | data formatting | bytes 6291456
  297.9 22.7 %all-to-all-done.2 = bf16[32,256,96]{1,2,0:T(8,128)(2,1)S(1)} async-done(((bf16[32,256,96]{1,2,0:T(8,128)(2,1)}), bf16[32,256,96]{1,2,0:T(8,128)(2,1)S(1)}, u32[]{:S(2)}, u32[]{:S(2)}) %all-to-all-start.2) | async-done | bytes 1572896 | tf_op jit(solution)/shard_map/all_to_all | solution.py:113
  320.7 2.4 copy.68
  323.1 13.0 %gather_fusion.1 = bf16[4096,96]{1,0:T(8,128)(2,1)S(1)} fusion(bf16[8192,96]{1,0:T(8,128)(2,1)} %bitcast.87, s32[4096]{0:T(1024)S(1)} %broadcast_clamp_fusion.1), kind=kCustom, calls=%fused_computation.1 | custom fusion | bytes 1589248 | tf_op jit(solution)/shard_map/gather | solution.py:120
  336.1 1.2 copy.70
  (54 shorter events, 8.6 us)
Async XLA Ops:
  0.6 36.8 %copy-start = (bf16[4096,256]{1,0:T(8,128)(2,1)S(1)}, bf16[4096,256]{1,0:T(8,128)(2,1)}, u32[]{:S(2)}) copy-start(bf16[4096,256]{1,0:T(8,128)(2,1)} %param.15) | copy-start | bytes 6291460
  30.2 24.8 %all-to-all-start = ((s32[32,1,256]{2,1,0:T(1,128)}), s32[32,1,256]{2,1,0:T(1,128)S(1)}, u32[]{:S(2)}, u32[]{:S(2)}) async-start(s32[32,1,256]{2,1,0:T(1,128)} %bitcast.5), calls=%async_computation | async-start | bytes 65536 | tf_op jit(solution)/shard_map/all_to_all | solution.py:78
  55.0 43.5 %all-to-all-start.1 = ((bf16[32,256,96]{1,2,0:T(8,128)(2,1)}), bf16[32,256,96]{1,2,0:T(8,128)(2,1)S(1)}, u32[]{:S(2)}, u32[]{:S(2)}) async-start(bf16[32,256,96]{1,2,0:T(8,128)(2,1)} %copy.52), calls=%async_computation.1 | async-start | bytes 3145728 | tf_op jit(solution)/shard_map/all_to_all | solution.py:71
  61.0 12.7 %copy-start.4 = (bf16[96,408]{1,0:T(8,128)(2,1)S(1)}, bf16[96,408]{1,0:T(8,128)(2,1)}, u32[]{:S(2)}) copy-start(bf16[96,408]{1,0:T(8,128)(2,1)} %param.13) | copy-start | bytes 235012
  61.1 12.7 %copy-start.6 = (f32[96]{0:T(128)S(1)}, f32[96]{0:T(128)}, u32[]{:S(2)}) copy-start(f32[96]{0:T(128)} %param.14) | copy-start | bytes 1156
  151.5 5.1 %copy-start.3 = (bf16[96,16384]{0,1:T(8,128)(2,1)}, bf16[96,16384]{0,1:T(8,128)(2,1)S(1)}, u32[]{:S(2)}) copy-start(bf16[96,16384]{0,1:T(8,128)(2,1)S(1)} %convert_element_type.36) | copy-start | bytes 9437188
  151.6 5.0 %collective-permute-start = (bf16[96,64,1]{0,1,2:T(8,128)(2,1)S(1)}, bf16[96,64,1]{0,1,2:T(8,128)(2,1)S(1)}, u32[]{:S(2)}, u32[]{:S(2)}) collective-permute-start(bf16[96,64,1]{0,1,2:T(8,128)(2,1)S(1)} %copy.78), channel_id=1, source_target_pairs={{0,4},{4,8},{8,12},{12,16},{16,20},{20,24},{24,28},{28,0},{1,5},{5... | collective-permute-start | bytes 36872 | tf_op jit(solution)/shard_map/ppermute | solution.py:14
  151.7 7.9 %collective-permute-start.1 = (bf16[96,64,1]{0,1,2:T(8,128)(2,1)S(1)}, bf16[96,64,1]{0,1,2:T(8,128)(2,1)S(1)}, u32[]{:S(2)}, u32[]{:S(2)}) collective-permute-start(bf16[96,64,1]{0,1,2:T(8,128)(2,1)S(1)} %copy.79), channel_id=1, source_target_pairs={{4,0},{8,4},{12,8},{16,12},{20,16},{24,20},{28,24},{0,28},{5,1},{9... | collective-permute-start | bytes 36872 | tf_op jit(solution)/shard_map/ppermute | solution.py:17
  159.9 6.0 %collective-permute-start.2 = (bf16[96,1,258]{0,1,2:T(2,128)(2,1)S(1)}, bf16[96,1,258]{0,1,2:T(2,128)(2,1)S(1)}, u32[]{:S(2)}, u32[]{:S(2)}) collective-permute-start(bf16[96,1,258]{0,1,2:T(2,128)(2,1)S(1)} %get-tuple-element.12), channel_id=1, source_target_pairs={{0,1},{1,2},{2,3},{4,5},{5,6},{6,7},{8,9},{9,10},{10,11},{12,13},{... | collective-permute-start | bytes 148616 | tf_op jit(solution)/shard_map/ppermute | solution.py:14
  163.4 6.9 %collective-permute-start.3 = (bf16[96,1,258]{0,1,2:T(2,128)(2,1)S(1)}, bf16[96,1,258]{0,1,2:T(2,128)(2,1)S(1)}, u32[]{:S(2)}, u32[]{:S(2)}) collective-permute-start(bf16[96,1,258]{0,1,2:T(2,128)(2,1)S(1)} %get-tuple-element.13), channel_id=1, source_target_pairs={{1,0},{2,1},{3,2},{5,4},{6,5},{7,6},{9,8},{10,9},{11,10},{13,12},{... | collective-permute-start | bytes 148616 | tf_op jit(solution)/shard_map/ppermute | solution.py:17
  174.4 0.9 copy-start.8
  174.4 0.9 copy-start.10
  185.9 1.9 copy-start.7
  190.8 5.0 %collective-permute-start.4 = (bf16[96,64,1]{0,1,2:T(8,128)(2,1)S(1)}, bf16[96,64,1]{0,1,2:T(8,128)(2,1)S(1)}, u32[]{:S(2)}, u32[]{:S(2)}) collective-permute-start(bf16[96,64,1]{0,1,2:T(8,128)(2,1)S(1)} %get-tuple-element.14), channel_id=1, source_target_pairs={{0,4},{4,8},{8,12},{12,16},{16,20},{20,24},{24,28},{28,0},{1,5},{5... | collective-permute-start | bytes 36872 | tf_op jit(solution)/shard_map/ppermute | solution.py:14
  190.9 5.0 %collective-permute-start.5 = (bf16[96,64,1]{0,1,2:T(8,128)(2,1)S(1)}, bf16[96,64,1]{0,1,2:T(8,128)(2,1)S(1)}, u32[]{:S(2)}, u32[]{:S(2)}) collective-permute-start(bf16[96,64,1]{0,1,2:T(8,128)(2,1)S(1)} %get-tuple-element.15), channel_id=1, source_target_pairs={{4,0},{8,4},{12,8},{16,12},{20,16},{24,20},{28,24},{0,28},{5,1},{9... | collective-permute-start | bytes 36872 | tf_op jit(solution)/shard_map/ppermute | solution.py:17
  196.2 6.8 %collective-permute-start.6 = (bf16[96,1,258]{0,1,2:T(2,128)(2,1)S(1)}, bf16[96,1,258]{0,1,2:T(2,128)(2,1)S(1)}, u32[]{:S(2)}, u32[]{:S(2)}) collective-permute-start(bf16[96,1,258]{0,1,2:T(2,128)(2,1)S(1)} %get-tuple-element.10), channel_id=1, source_target_pairs={{0,1},{1,2},{2,3},{4,5},{5,6},{6,7},{8,9},{9,10},{10,11},{12,13},{... | collective-permute-start | bytes 148616 | tf_op jit(solution)/shard_map/ppermute | solution.py:14
  200.5 6.9 %collective-permute-start.7 = (bf16[96,1,258]{0,1,2:T(2,128)(2,1)S(1)}, bf16[96,1,258]{0,1,2:T(2,128)(2,1)S(1)}, u32[]{:S(2)}, u32[]{:S(2)}) collective-permute-start(bf16[96,1,258]{0,1,2:T(2,128)(2,1)S(1)} %get-tuple-element.11), channel_id=1, source_target_pairs={{1,0},{2,1},{3,2},{5,4},{6,5},{7,6},{9,8},{10,9},{11,10},{13,12},{... | collective-permute-start | bytes 148616 | tf_op jit(solution)/shard_map/ppermute | solution.py:17
  214.2 0.9 copy-start.9
  227.6 3.3 copy-start.2
  231.0 15.8 %slice-start = ((s8[8388608]{0:T(1024)(128)(4,1)}), s8[4194304]{0:T(1024)(128)(4,1)S(1)}, s32[]{:S(2)}) async-start(s8[8388608]{0:T(1024)(128)(4,1)} %bitcast.82), calls=%async_computation.3 | async-start | bytes 8388608
  235.1 11.7 %slice-start.1 = ((s8[8388608]{0:T(1024)(128)(4,1)}), s8[4194304]{0:T(1024)(128)(4,1)S(1)}, s32[]{:S(2)}) async-start(s8[8388608]{0:T(1024)(128)(4,1)} %bitcast.82), calls=%async_computation.4 | async-start | bytes 8388608
  235.1 11.7 %copy-start.5 = (f32[96]{0:T(128)S(1)}, f32[96]{0:T(128)}, u32[]{:S(2)}) copy-start(f32[96]{0:T(128)} %param.23) | copy-start | bytes 1156
  279.7 41.0 %all-to-all-start.2 = ((bf16[32,256,96]{1,2,0:T(8,128)(2,1)}), bf16[32,256,96]{1,2,0:T(8,128)(2,1)S(1)}, u32[]{:S(2)}, u32[]{:S(2)}) async-start(bf16[32,256,96]{1,2,0:T(8,128)(2,1)} %copy.67), calls=%async_computation.2 | async-start | bytes 3145728 | tf_op jit(solution)/shard_map/all_to_all | solution.py:113
  323.1 14.3 %copy-start.1 = (bf16[4096,256]{1,0:T(8,128)(2,1)S(1)}, bf16[4096,256]{1,0:T(8,128)(2,1)}, u32[]{:S(2)}) copy-start(bf16[4096,256]{1,0:T(8,128)(2,1)} %param.15) | copy-start | bytes 6291460
where the time goes:
time: 344 us; the launch traced here: 338 us
  local copies, waits for them, and re-layouts  138 us (40%)
  other arithmetic  88.2 us (26%)
  waiting for transfers between devices  46.9 us (14%)
  starting transfers between devices  34.4 us (10%)
  matrix products  28.8 us (8%)
    scatter-add x1, other arithmetic, on_device(): mapped_features.at[:, scatter_cell]  46.4 us
    unnamed x33, local copies, waits for them, and re-layouts  27.8 us
    gather x1, local copies, waits for them, and re-layouts, on_device(): picked = corrected.reshape(features, mesh_point_total)[:, read_cell].T  24.6 us
    all_to_all x1, waiting for transfers between devices, on_device(): lax.all_to_all(picked.reshape(devices, capacity, features), ('lon', 'lat'...  22.7 us
    conv_general_dilated x2, matrix products, conv_valid(): lax.conv_general_dilated(field[None], kernel, (1, 1), 'VALID', dimension_...  21.2 us
    conv_general_dilated x8, local copies, waits for them, and re-layouts, conv_valid(): lax.conv_general_dilated(field[None], kernel, (1, 1), 'VALID', dimension_...  20.8 us
    scatter x1, local copies, waits for them, and re-layouts, on_device(): jnp.full((slot_total,), -1, jnp.int32).at[position]  16.3 us
    convert_element_type x2, other arithmetic, on_device(): (merged.astype(jnp.float32) + second + latter_filter_offset[:, None, None...  13.2 us
  transfers between devices with their start and end apart: 11, of which 8 were waited for; matrix products, arithmetic and copies ran while one was open for 18% of the time, Pallas kernels for 0%

commit v1 on v0

v1 whole, which is shorter than its diff:
```python
import functools

import jax
import jax.numpy as jnp
from jax import lax
from jax.experimental import pallas as pl
from jax.experimental.pallas import tpu as pltpu
from jax.sharding import PartitionSpec as P

LANES = 128
EDGE = 16
VMEM_BYTES = 56 * 1024 * 1024

VMEM = pl.BlockSpec(memory_space=pltpu.VMEM)
SMEM = pl.BlockSpec(memory_space=pltpu.SMEM)


def params():
    return pltpu.CompilerParams(vmem_limit_bytes=VMEM_BYTES)


def route_kernel(features, columns, pos_ref, cell_ref, rec_ref, w_ref, off_ref, out_ref, emb, slots):
    rows = rec_ref.shape[0]
    total = out_ref.shape[0]

    @pl.loop(0, total // 128)
    def _(b):
        slots[pl.ds(pl.multiple_of(b * 128, 128), 128), :] = jnp.zeros((128, LANES), jnp.float32)

    lane = lax.broadcasted_iota(jnp.int32, (128, LANES), 1)

    @pl.loop(0, rows // 128)
    def _(b):
        at = pl.ds(pl.multiple_of(b * 128, 128), 128)
        e = jnp.dot(rec_ref[at, :], w_ref[...], preferred_element_type=jnp.float32) + off_ref[...]
        e = e.astype(jnp.bfloat16).astype(jnp.float32)
        cell = jnp.broadcast_to(cell_ref[pl.ds(b, 1), :], (128, 128)).T
        line = (cell // columns + 1).astype(jnp.float32)
        place = (cell % columns).astype(jnp.float32)
        e = jnp.where(lane == features, line, jnp.where(lane == features + 1, place, e))
        emb[at, :] = e

    @pl.loop(0, rows // 16)
    def _(b):
        for j in range(16):
            i = b * 16 + j
            slots[pl.ds(pos_ref[i], 1), :] = emb[pl.ds(i, 1), :]

    @pl.loop(0, total // 128)
    def _(b):
        at = pl.ds(pl.multiple_of(b * 128, 128), 128)
        out_ref[at, :] = slots[at, :].astype(jnp.bfloat16)


def merge_kernel(cell_ref, proj_ref, arr_ref, out_ref, rows32, s1, s2, s3, s0):
    total = arr_ref.shape[0]
    cells = proj_ref.shape[0]

    @pl.loop(0, total // 128)
    def _(b):
        at = pl.ds(pl.multiple_of(b * 128, 128), 128)
        rows32[at, :] = arr_ref[at, :].astype(jnp.float32)

    @pl.loop(0, cells // 128)
    def _(b):
        at = pl.ds(pl.multiple_of(b * 128, 128), 128)
        for s in (s0, s1, s2, s3):
            s[at, :] = jnp.zeros((128, LANES), jnp.float32)

    sums = (s0, s1, s2, s3)

    @pl.loop(0, total // 16)
    def _(b):
        for g in range(4):
            idx = [b * 16 + g * 4 + j for j in range(4)]
            at = [pl.ds(cell_ref[i], 1) for i in idx]
            new = [sums[j][at[j], :] + rows32[pl.ds(idx[j], 1), :] for j in range(4)]
            for j in range(4):
                sums[j][at[j], :] = new[j]

    @pl.loop(0, cells // 128)
    def _(b):
        at = pl.ds(pl.multiple_of(b * 128, 128), 128)
        out_ref[at, :] = (
            proj_ref[at, :] + ((s0[at, :] + s1[at, :]) + (s2[at, :] + s3[at, :]))
        ).astype(jnp.bfloat16)


def pair_dot(patches, row, width, w_ref):
    y = None
    for dr in range(4):
        lhs = jnp.concatenate([patches[row + dr, k, pl.ds(0, width), :] for k in range(3)], axis=1)
        part = jnp.dot(lhs, w_ref[pl.ds(dr * 384, 384), :], preferred_element_type=jnp.float32)
        y = part if y is None else y + part
    return y


def conv_kernel(
    features, ends_ref, cell_ref, m_ref, left_ref, right_ref, top_ref, bottom_ref,
    w1_ref, b1_ref, w2_ref, b2_ref, out_ref, got_ref, patches, wide, corr, stage,
):
    height, width, _ = m_ref.shape
    tall = width + EDGE

    def spread(row):
        for k in range(3):
            patches[row, k, :, :] = wide[pl.ds(EDGE - 2 + k, tall), :].astype(jnp.bfloat16)

    for ref, base in ((top_ref, 0), (bottom_ref, height + 2)):
        for t in range(2):
            wide[...] = ref[t].astype(jnp.float32)
            spread(base + t)

    @pl.loop(0, height)
    def _(r):
        wide[pl.ds(0, EDGE), :] = left_ref[r].astype(jnp.float32)
        wide[pl.ds(EDGE, width), :] = m_ref[r].astype(jnp.float32)
        wide[pl.ds(EDGE + width, EDGE), :] = right_ref[r].astype(jnp.float32)
        spread(r + 2)

    @pl.loop(0, height // 2 + 1)
    def _(p):
        y = pair_dot(patches, 2 * p, tall, w1_ref) + b1_ref[...]
        hidden = jax.nn.gelu(y)
        for t in range(2):
            h = 2 * p + t
            outside = ((h == 0) & (ends_ref[0] == 1)) | ((h == height + 1) & (ends_ref[1] == 1))
            part = hidden[:, t * LANES:(t + 1) * LANES]
            wide[pl.ds(0, tall), :] = jnp.where(outside, 0.0, part)
            for k in range(3):
                patches[h, k, pl.ds(0, width), :] = wide[pl.ds(k, width), :].astype(jnp.bfloat16)

    @pl.loop(0, height // 2)
    def _(p):
        y = pair_dot(patches, 2 * p, width, w2_ref) + b2_ref[...]
        for t in range(2):
            r = 2 * p + t
            v = m_ref[r].astype(jnp.float32) + y[:, t * LANES:(t + 1) * LANES]
            corr[pl.ds(pl.multiple_of(r * width, 128), width), :] = v
            out_ref[r] = v.T[:features].astype(jnp.bfloat16)

    total = got_ref.shape[0]

    @pl.loop(0, total // 16)
    def _(b):
        for j in range(16):
            i = b * 16 + j
            stage[pl.ds(i, 1), :] = corr[pl.ds(cell_ref[i], 1), :]

    @pl.loop(0, total // 128)
    def _(b):
        at = pl.ds(pl.multiple_of(b * 128, 128), 128)
        got_ref[at, :] = stage[at, :].astype(jnp.bfloat16)


def return_kernel(features, pos_ref, got_ref, out_ref, rows32, stage):
    total = got_ref.shape[0]
    rows = out_ref.shape[0]

    @pl.loop(0, total // 128)
    def _(b):
        at = pl.ds(pl.multiple_of(b * 128, 128), 128)
        rows32[at, :] = got_ref[at, :].astype(jnp.float32)

    @pl.loop(0, rows // 16)
    def _(b):
        for j in range(16):
            i = b * 16 + j
            stage[pl.ds(i, 1), :] = rows32[pl.ds(pos_ref[i], 1), :]

    @pl.loop(0, rows // 128)
    def _(b):
        at = pl.ds(pl.multiple_of(b * 128, 128), 128)
        out_ref[at, :] = stage[at, :][:, :features].astype(jnp.bfloat16)


def slots_of(tile, devices, capacity):
    block = 128
    hot = (tile.reshape(-1, block)[:, :, None] == jnp.arange(devices, dtype=jnp.int32)).astype(
        jnp.bfloat16
    )
    below = jnp.tril(jnp.ones((block, block), jnp.bfloat16), -1)
    inside = jnp.einsum("ij,bjd->bid", below, hot, preferred_element_type=jnp.float32)
    totals = jnp.sum(hot.astype(jnp.float32), axis=1)
    blocks = totals.shape[0]
    before = jnp.sum(
        jnp.where(
            (jnp.arange(blocks)[:, None] > jnp.arange(blocks)[None, :])[:, :, None],
            totals[None],
            0.0,
        ),
        axis=1,
    )
    rank = jnp.sum((inside + before[:, None, :]) * hot.astype(jnp.float32), axis=2)
    return tile * capacity + rank.reshape(-1).astype(jnp.int32)


def pair_weights(kernel):
    out, into = kernel.shape[:2]
    k = jnp.pad(
        jnp.transpose(kernel, (2, 3, 1, 0)), ((0, 0), (0, 0), (0, LANES - into), (0, LANES - out))
    )
    rest = ((0, 0), (0, 0), (0, 0))
    both = jnp.concatenate(
        [jnp.pad(k, ((0, 1),) + rest), jnp.pad(k, ((1, 0),) + rest)], axis=3
    )
    return both.reshape(4 * 3 * LANES, 2 * LANES)


def pair_bias(bias):
    padded = jnp.pad(bias, (0, LANES - bias.shape[0]))
    return jnp.concatenate([padded, padded])[None]


def on_device(
    ensemble_prediction,
    mapping_matrix,
    mapping_offset,
    gauge_measured_records,
    gauge_scatter_matrix,
    gauge_scatter_offset,
    gauge_block_number,
    gauge_point_position,
    initial_filter_matrix,
    initial_filter_offset,
    latter_filter_matrix,
    latter_filter_offset,
):
    depth, height, width = ensemble_prediction.shape
    features = mapping_matrix.shape[0]
    more = LANES - features
    cells = height * width
    lon_size = lax.axis_size("lon")
    lat_size = lax.axis_size("lat")
    devices = lon_size * lat_size
    held_rows = gauge_measured_records.shape[0]
    capacity = 2 * held_rows // devices
    slot_total = devices * capacity
    f32, bf16 = jnp.float32, jnp.bfloat16

    def exchange(rows):
        return lax.all_to_all(
            rows.reshape(devices, capacity, LANES),
            ("lon", "lat"),
            split_axis=0,
            concat_axis=0,
            tiled=True,
        ).reshape(slot_total, LANES)

    position = slots_of(gauge_block_number[:, 0], devices, capacity)
    payload = pl.pallas_call(
        functools.partial(route_kernel, features, width),
        out_shape=jax.ShapeDtypeStruct((slot_total, LANES), bf16),
        in_specs=[SMEM, VMEM, VMEM, VMEM, VMEM],
        out_specs=VMEM,
        scratch_shapes=[
            pltpu.VMEM((held_rows, LANES), f32),
            pltpu.VMEM((slot_total, LANES), f32),
        ],
        compiler_params=params(),
        name="route",
    )(
        position,
        gauge_point_position.reshape(-1, 128),
        gauge_measured_records,
        jnp.pad(gauge_scatter_matrix, ((0, 0), (0, more))),
        jnp.pad(gauge_scatter_offset, (0, more))[None],
    )
    arrived = exchange(payload)
    line = arrived[:, features].astype(jnp.int32)
    place = arrived[:, features + 1].astype(jnp.int32)
    cell = jnp.clip((line - 1) * width + place, 0, cells - 1)

    projected = lax.dot_general(
        ensemble_prediction.reshape(depth, cells),
        jnp.pad(mapping_matrix, ((0, more), (0, 0))),
        (((0,), (1,)), ((), ())),
        preferred_element_type=f32,
    ) + jnp.pad(mapping_offset, (0, more))[None]

    field = pltpu.VMEM((cells, LANES), f32)
    merged = pl.pallas_call(
        merge_kernel,
        out_shape=jax.ShapeDtypeStruct((cells, LANES), bf16),
        in_specs=[SMEM, VMEM, VMEM],
        out_specs=VMEM,
        scratch_shapes=[pltpu.VMEM((slot_total, LANES), f32)] + [field] * 4,
        compiler_params=params(),
        name="merge",
    )(cell, projected, arrived).reshape(height, width, LANES)

    around = [(i, (i + 1) % lon_size) for i in range(lon_size)]
    back = [(b, a) for a, b in around]
    left = lax.ppermute(merged[:, width - EDGE:], "lon", around)
    right = lax.ppermute(merged[:, :EDGE], "lon", back)
    down = [(i, i + 1) for i in range(lat_size - 1)]
    up = [(b, a) for a, b in down]

    def strip(at):
        return jnp.concatenate([left[at], merged[at], right[at]], axis=1)

    top = lax.ppermute(strip(slice(height - 2, height)), "lat", down)
    bottom = lax.ppermute(strip(slice(0, 2)), "lat", up)
    me = lax.axis_index("lat")
    ends = jnp.stack([(me == 0).astype(jnp.int32), (me == lat_size - 1).astype(jnp.int32)])

    corrected, picked = pl.pallas_call(
        functools.partial(conv_kernel, features),
        out_shape=(
            jax.ShapeDtypeStruct((height, features, width), bf16),
            jax.ShapeDtypeStruct((slot_total, LANES), bf16),
        ),
        in_specs=[SMEM, SMEM] + [VMEM] * 9,
        out_specs=(VMEM, VMEM),
        scratch_shapes=[
            pltpu.VMEM((height + 4, 3, width + EDGE, LANES), bf16),
            pltpu.VMEM((width + 2 * EDGE, LANES), f32),
            pltpu.VMEM((cells, LANES), f32),
            pltpu.VMEM((slot_total, LANES), f32),
        ],
        compiler_params=params(),
        name="convs",
    )(
        ends,
        cell,
        merged,
        left,
        right,
        top,
        bottom,
        pair_weights(initial_filter_matrix),
        pair_bias(initial_filter_offset),
        pair_weights(latter_filter_matrix),
        pair_bias(latter_filter_offset),
    )

    station_values = pl.pallas_call(
        functools.partial(return_kernel, features),
        out_shape=jax.ShapeDtypeStruct((held_rows, features), bf16),
        in_specs=[SMEM, VMEM],
        out_specs=VMEM,
        scratch_shapes=[
            pltpu.VMEM((slot_total, LANES), f32),
            pltpu.VMEM((held_rows, LANES), f32),
        ],
        compiler_params=params(),
        name="unroute",
    )(position, exchange(picked))
    return (jnp.transpose(corrected, (1, 0, 2)), station_values)


def solution(mesh):
    placed = (
        P(None, "lat", "lon"),
        P(),
        P(),
        P(("lon", "lat"), None),
        P(),
        P(),
        P(("lon", "lat"), None),
        P(("lon", "lat")),
        P(),
        P(),
        P(),
        P(),
    )
    return jax.shard_map(
        on_device,
        mesh=mesh,
        in_specs=placed,
        out_specs=(P(None, "lat", "lon"), P(("lon", "lat"), None)),
        check_vma=False,
    )
```

time: 344 us -> 245 us (0.71); the launches traced: 338 us -> 244 us
  local copies, waits for them, and re-layouts: 138 us -> 31.8 us
  Pallas kernels: 0 us -> 96.9 us
  other arithmetic: 88.2 us -> 9.13 us
  waiting for transfers between devices: 46.9 us -> 66.2 us
  matrix products: 28.8 us -> 15.8 us
  starting transfers between devices: 34.4 us -> 23.5 us
    pallas_call x0 -> x4, Pallas kernels: none -> 96.9 us  [the longest x1 51.9 us: on_device(): pl.pallas_call(functools.partial(conv_kernel, features), out_shape=(jax.S...]
    scatter-add x1 -> x0, other arithmetic: 46.4 us -> none  [on_device(): mapped_features.at[:, scatter_cell]]
    gather x2 -> x0, local copies, waits for them, and re-layouts: 37.6 us -> none  [the longest x1 24.6 us: on_device(): picked = corrected.reshape(features, mesh_point_total)[:, read_cell].T]
    all_to_all x3 -> x2, waiting for transfers between devices: 32.9 us -> 61.1 us  [exchange(): lax.all_to_all(rows.reshape(devices, capacity, LANES), ('lon', 'lat'), sp...]
    scatter x2 -> x0, local copies, waits for them, and re-layouts: 28.1 us -> none  [the longest x1 16.3 us: on_device(): jnp.full((slot_total,), -1, jnp.int32).at[position]]
    conv_general_dilated x2 -> x0, matrix products: 21.2 us -> none  [conv_valid(): lax.conv_general_dilated(field[None], kernel, (1, 1), 'VALID', dimension_...]
    convert_element_type x5 -> x0, other arithmetic: 20.9 us -> none  [the longest x2 13.2 us: on_device(): (merged.astype(jnp.float32) + second + latter_filter_offset[:, None, None...]
    conv_general_dilated x8 -> x0, local copies, waits for them, and re-layouts: 20.8 us -> none  [conv_valid(): lax.conv_general_dilated(field[None], kernel, (1, 1), 'VALID', dimension_...]
  transfers between devices with their start and end apart: 11 -> 6, of which waited for: 8 -> 5; matrix products, arithmetic and copies ran while one was open for 18% -> 17% of each run, Pallas kernels for 0% -> 0%
where the time goes in v1:
time: 245 us; the launch traced here: 244 us
  Pallas kernels  96.9 us (40%)
  waiting for transfers between devices  66.2 us (27%)
  local copies, waits for them, and re-layouts  31.8 us (13%)
  starting transfers between devices  23.5 us (10%)
  matrix products  15.8 us (6%)
  other arithmetic  9.13 us (4%)
    all_to_all x2, waiting for transfers between devices, exchange(): lax.all_to_all(rows.reshape(devices, capacity, LANES), ('lon', 'lat'), sp...  61.1 us
    pallas_call x1, Pallas kernels, on_device(): pl.pallas_call(functools.partial(conv_kernel, features), out_shape=(jax.S...  51.9 us
    unnamed x30, local copies, waits for them, and re-layouts  25.4 us
    pallas_call x1, Pallas kernels, on_device(): pl.pallas_call(merge_kernel, out_shape=jax.ShapeDtypeStruct((cells, LANES...  23.7 us
    dot_general x1, matrix products, on_device(): lax.dot_general(ensemble_prediction.reshape(depth, cells), jnp.pad(mappin...  14.7 us
    pallas_call x1, Pallas kernels, on_device(): pl.pallas_call(functools.partial(route_kernel, features, width), out_shap...  13.5 us
    all_to_all x2, starting transfers between devices, exchange(): lax.all_to_all(rows.reshape(devices, capacity, LANES), ('lon', 'lat'), sp...  13.2 us
    pallas_call x1, Pallas kernels, on_device(): pl.pallas_call(functools.partial(return_kernel, features), out_shape=jax....  7.87 us
  transfers between devices with their start and end apart: 6, of which 5 were waited for; matrix products, arithmetic and copies ran while one was open for 17% of the time, Pallas kernels for 0%

profile of v1, /device:TPU:0, one launch (start us, length us, event | category | flops | bytes accessed | tf_op | source)
XLA Modules:
  0.0 244.1 jit_solution(2430374946507397635)
XLA Ops:
  0.7 0.7 broadcast_multiply_fusion
  1.4 0.9 convert_reduce_fusion
  2.3 0.9 copy.32
  3.2 1.2 pad_bitcast_fusion.off_ref
  4.5 0.2 select_reduce_fusion
  4.7 1.1 fusion.7
  5.8 0.6 bitcast_add_fusion.pos_ref
  6.4 0.6 pad.42.w_ref
  7.1 13.5 %route.1 = bf16[8192,128]{1,0:T(8,128)(2,1)} custom-call(s32[4096]{0:T(1024)} %bitcast_add_fusion.pos_ref, s32[32,128]{1,0:T(8,128)} %bitcast.56, bf16[4096,256]{1,0:T(8,128)(2,1)} %rec_ref.1, bf16[256,128]{1,0:T(8,128)(2,1)} %pad.42.w_ref, f32[1,128]{1,0:T(1,128)} %pad_bitcast_fusion.off_ref), custom_call_target="tpu_custom_call" | custom-call | tf_op jit(solution)/shard_map/route/pallas_call | solution.py:251
  20.5 7.3 %all-to-all-start = ((bf16[32,256,128]{2,1,0:T(8,128)(2,1)}), bf16[32,256,128]{2,1,0:T(8,128)(2,1)S(1)}, u32[]{:S(2)}, u32[]{:S(2)}) async-start(bf16[32,256,128]{2,1,0:T(8,128)(2,1)} %bitcast.43), calls=%async_computation | async-start | bytes 4194304 | tf_op jit(solution)/shard_map/all_to_all | solution.py:242
  27.8 0.0 copy-start.5
  27.8 0.0 copy-start.6
  27.9 0.0 copy-start.10
  27.9 0.0 copy-start.11
  27.9 0.0 copy-start.9
  27.9 14.9 %copy.41 = bf16[51,8,64,256]{3,1,2,0:T(8,128)(2,1)} copy(bf16[51,8,64,256]{3,2,1,0:T(8,128)(2,1)} %bitcast.42) | data formatting | bytes 26738688
  42.8 0.1 pad.46
  42.9 0.0 copy-done.6
  42.9 0.1 pad.50
  43.0 0.1 fusion.8
  43.1 1.1 fusion.9
  44.2 14.7 %fusion.proj_ref = f32[16384,128]{1,0:T(8,128)} fusion(bf16[408,16384]{1,0:T(8,128)(2,1)} %bitcast.37, f32[128]{0:T(128)S(1)} %pad.45, bf16[96,408]{1,0:T(8,128)(2,1)S(1)} %copy-done.9), kind=kOutput, calls=%fused_computation.1 | convolution fusion | flops 1713373184 | bytes 21836800 | tf_op jit(solution)/shard_map/dot_general | solution.py:274
  58.8 17.7 %all-to-all-done = bf16[32,256,128]{2,1,0:T(8,128)(2,1)S(1)} async-done(((bf16[32,256,128]{2,1,0:T(8,128)(2,1)}), bf16[32,256,128]{2,1,0:T(8,128)(2,1)S(1)}, u32[]{:S(2)}, u32[]{:S(2)}) %all-to-all-start) | async-done | bytes 2097184 | tf_op jit(solution)/shard_map/all_to_all | solution.py:242
  76.5 3.7 %clamp_reduce_fusion.cell_ref = s32[8192]{0:T(1024)} fusion(bf16[8192,128]{1,0:T(8,128)(2,1)S(1)} %bitcast.38), kind=kLoop, calls=%fused_computation.2 | loop fusion | flops 49152 | bytes 65536 | tf_op jit(solution)/shard_map/jit(clip)/min | solution.py:272
  80.3 23.7 %merge.1 = bf16[16384,128]{1,0:T(8,128)(2,1)} custom-call(s32[8192]{0:T(1024)} %clamp_reduce_fusion.cell_ref, f32[16384,128]{1,0:T(8,128)} %fusion.proj_ref, bf16[8192,128]{1,0:T(8,128)(2,1)} %bitcast.39), custom_call_target="tpu_custom_call" | custom-call | tf_op jit(solution)/shard_map/merge/pallas_call | solution.py:282
  104.0 1.1 fusion.23
  105.1 0.9 collective-permute-start
  106.0 0.6 pad_maximum_fusion.2
  106.6 3.5 %collective-permute-start.1 = (bf16[64,16,128]{2,1,0:T(8,128)(2,1)S(1)}, bf16[64,16,128]{2,1,0:T(8,128)(2,1)S(1)}, u32[]{:S(2)}, u32[]{:S(2)}) collective-permute-start(bf16[64,16,128]{2,1,0:T(8,128)(2,1)S(1)} %get-tuple-element.16), channel_id=1, source_target_pairs={{4,0},{8,4},{12,8},{16,12},{20,16},{24,20},{28,24},{0,28},{5,1},{9... | collective-permute-start | bytes 786440 | tf_op jit(solution)/shard_map/ppermute | solution.py:295
  110.1 1.0 fusion.22
  111.1 2.9 %collective-permute-done.left_ref = bf16[64,16,128]{2,1,0:T(8,128)(2,1)S(1)} collective-permute-done((bf16[64,16,128]{2,1,0:T(8,128)(2,1)S(1)}, bf16[64,16,128]{2,1,0:T(8,128)(2,1)S(1)}, u32[]{:S(2)}, u32[]{:S(2)}) %collective-permute-start) | collective-permute-done | bytes 262176 | tf_op jit(solution)/shard_map/ppermute | solution.py:294
  114.0 1.6 collective-permute-done.1.right_ref
  115.6 1.3 collective-permute-start.3
  116.9 4.6 %collective-permute-start.2 = (bf16[2,288,128]{2,1,0:T(8,128)(2,1)S(1)}, bf16[2,288,128]{2,1,0:T(8,128)(2,1)S(1)}, u32[]{:S(2)}, u32[]{:S(2)}) collective-permute-start(bf16[2,288,128]{2,1,0:T(8,128)(2,1)S(1)} %pad_maximum_fusion), channel_id=1, source_target_pairs={{0,1},{1,2},{2,3},{4,5},{5,6},{6,7},{8,9},{9,10},{10,11},{12,13},{... | collective-permute-start | bytes 442376 | tf_op jit(solution)/shard_map/ppermute | solution.py:302
  121.5 0.6 add_convert_fusion.ends_ref
  122.0 1.2 copy.35
  123.2 1.2 copy.36
  124.4 0.5 pad_maximum_fusion.3
  124.9 0.0 collective-permute-done.3.bottom_ref
  124.9 0.7 collective-permute-done.2.top_ref
  125.6 0.6 copy-done.8
  126.2 51.9 %convs.1 = (bf16[64,96,256]{2,1,0:T(8,128)(2,1)}, bf16[8192,128]{1,0:T(8,128)(2,1)}) custom-call(s32[2]{0:T(128)} %add_convert_fusion.ends_ref, s32[8192]{0:T(1024)} %clamp_reduce_fusion.cell_ref, bf16[64,256,128]{2,1,0:T(8,128)(2,1)} %bitcast.41, bf16[64,16,128]{2,1,0:T(8,128)(2,1)} %copy-done.3, bf16[64,16,128]{2,1,0:T(8,128)(2,1)} %copy-done.4, ...), custom_call_target="tpu_custom_call" | custom-call | tf_op jit(solution)/shard_map/convs/pallas_call | solution.py:307
  178.1 5.9 %all-to-all-start.1 = ((bf16[32,256,128]{2,1,0:T(8,128)(2,1)}), bf16[32,256,128]{2,1,0:T(8,128)(2,1)S(1)}, u32[]{:S(2)}, u32[]{:S(2)}) async-start(bf16[32,256,128]{2,1,0:T(8,128)(2,1)} %bitcast.48), calls=%async_computation.1 | async-start | bytes 4194304 | tf_op jit(solution)/shard_map/all_to_all | solution.py:242
  184.0 5.3 %copy.37 = bf16[96,64,256]{2,1,0:T(8,128)(2,1)} copy(bf16[96,64,256]{2,0,1:T(8,128)(2,1)} %bitcast.47) | data formatting | bytes 6291456
  189.3 43.4 %all-to-all-done.1 = bf16[32,256,128]{2,1,0:T(8,128)(2,1)S(1)} async-done(((bf16[32,256,128]{2,1,0:T(8,128)(2,1)}), bf16[32,256,128]{2,1,0:T(8,128)(2,1)S(1)}, u32[]{:S(2)}, u32[]{:S(2)}) %all-to-all-start.1) | async-done | bytes 2097184 | tf_op jit(solution)/shard_map/all_to_all | solution.py:242
  232.7 1.3 copy-done.1
  234.0 7.9 %unroute.1 = bf16[4096,96]{1,0:T(8,128)(2,1)} custom-call(s32[4096]{0:T(1024)} %bitcast_add_fusion.pos_ref, bf16[8192,128]{1,0:T(8,128)(2,1)} %bitcast.44), custom_call_target="tpu_custom_call" | custom-call | tf_op jit(solution)/shard_map/unroute/pallas_call | solution.py:337
  241.9 2.2 copy.38
  (27 shorter events, 0.1 us)
Async XLA Ops:
  20.5 56.0 %all-to-all-start = ((bf16[32,256,128]{2,1,0:T(8,128)(2,1)}), bf16[32,256,128]{2,1,0:T(8,128)(2,1)S(1)}, u32[]{:S(2)}, u32[]{:S(2)}) async-start(bf16[32,256,128]{2,1,0:T(8,128)(2,1)} %bitcast.43), calls=%async_computation | async-start | bytes 4194304 | tf_op jit(solution)/shard_map/all_to_all | solution.py:242
  27.8 15.0 %copy-start.5 = (bf16[96,96,3,3]{1,0,3,2:T(8,128)(2,1)S(1)}, bf16[96,96,3,3]{1,0,3,2:T(8,128)(2,1)}, u32[]{:S(2)}) copy-start(bf16[96,96,3,3]{1,0,3,2:T(8,128)(2,1)} %param.20) | copy-start | bytes 497668
  27.8 15.0 %copy-start.6 = (bf16[96,96,3,3]{1,0,3,2:T(8,128)(2,1)S(1)}, bf16[96,96,3,3]{1,0,3,2:T(8,128)(2,1)}, u32[]{:S(2)}) copy-start(bf16[96,96,3,3]{1,0,3,2:T(8,128)(2,1)} %param.22) | copy-start | bytes 497668
  27.9 15.1 %copy-start.10 = (f32[96]{0:T(128)S(1)}, f32[96]{0:T(128)}, u32[]{:S(2)}) copy-start(f32[96]{0:T(128)} %param.14) | copy-start | bytes 1156
  27.9 15.1 %copy-start.11 = (f32[96]{0:T(128)S(1)}, f32[96]{0:T(128)}, u32[]{:S(2)}) copy-start(f32[96]{0:T(128)} %param.21) | copy-start | bytes 1156
  27.9 16.3 %copy-start.9 = (bf16[96,408]{1,0:T(8,128)(2,1)S(1)}, bf16[96,408]{1,0:T(8,128)(2,1)}, u32[]{:S(2)}) copy-start(bf16[96,408]{1,0:T(8,128)(2,1)} %param.13) | copy-start | bytes 235012
  76.5 3.7 %copy-start = (bf16[32,256,128]{2,1,0:T(8,128)(2,1)}, bf16[32,256,128]{2,1,0:T(8,128)(2,1)S(1)}, u32[]{:S(2)}) copy-start(bf16[32,256,128]{2,1,0:T(8,128)(2,1)S(1)} %all-to-all-done) | copy-start | bytes 6291460
  104.0 19.2 %copy-start.2 = (bf16[4,3,128,256]{2,3,1,0:T(8,128)(2,1)S(1)}, bf16[4,3,128,256]{2,3,1,0:T(8,128)(2,1)}, u32[]{:S(2)}) copy-start(bf16[4,3,128,256]{2,3,1,0:T(8,128)(2,1)} %fusion.9) | copy-start | bytes 2359300
  104.0 20.4 %copy-start.12 = (f32[96]{0:T(128)S(1)}, f32[96]{0:T(128)}, u32[]{:S(2)}) copy-start(f32[96]{0:T(128)} %param.23) | copy-start | bytes 1156
  105.1 8.9 %collective-permute-start = (bf16[64,16,128]{2,1,0:T(8,128)(2,1)S(1)}, bf16[64,16,128]{2,1,0:T(8,128)(2,1)S(1)}, u32[]{:S(2)}, u32[]{:S(2)}) collective-permute-start(bf16[64,16,128]{2,1,0:T(8,128)(2,1)S(1)} %get-tuple-element.17), channel_id=1, source_target_pairs={{0,4},{4,8},{8,12},{12,16},{16,20},{20,24},{24,28},{28,0},{1,5},{5... | collective-permute-start | bytes 786440 | tf_op jit(solution)/shard_map/ppermute | solution.py:294
  106.6 9.0 %collective-permute-start.1 = (bf16[64,16,128]{2,1,0:T(8,128)(2,1)S(1)}, bf16[64,16,128]{2,1,0:T(8,128)(2,1)S(1)}, u32[]{:S(2)}, u32[]{:S(2)}) collective-permute-start(bf16[64,16,128]{2,1,0:T(8,128)(2,1)S(1)} %get-tuple-element.16), channel_id=1, source_target_pairs={{4,0},{8,4},{12,8},{16,12},{20,16},{24,20},{28,24},{0,28},{5,1},{9... | collective-permute-start | bytes 786440 | tf_op jit(solution)/shard_map/ppermute | solution.py:295
  114.0 11.6 %copy-start.3 = (bf16[64,16,128]{2,1,0:T(8,128)(2,1)}, bf16[64,16,128]{2,1,0:T(8,128)(2,1)S(1)}, u32[]{:S(2)}) copy-start(bf16[64,16,128]{2,1,0:T(8,128)(2,1)S(1)} %collective-permute-done.left_ref) | copy-start | bytes 786436
  115.6 10.0 %copy-start.4 = (bf16[64,16,128]{2,1,0:T(8,128)(2,1)}, bf16[64,16,128]{2,1,0:T(8,128)(2,1)S(1)}, u32[]{:S(2)}) copy-start(bf16[64,16,128]{2,1,0:T(8,128)(2,1)S(1)} %collective-permute-done.1.right_ref) | copy-start | bytes 786436
  115.6 9.3 %collective-permute-start.3 = (bf16[2,288,128]{2,1,0:T(8,128)(2,1)S(1)}, bf16[2,288,128]{2,1,0:T(8,128)(2,1)S(1)}, u32[]{:S(2)}, u32[]{:S(2)}) collective-permute-start(bf16[2,288,128]{2,1,0:T(8,128)(2,1)S(1)} %pad_maximum_fusion.1), channel_id=1, source_target_pairs={{1,0},{2,1},{3,2},{5,4},{6,5},{7,6},{9,8},{10,9},{11,10},{13,12},{... | collective-permute-start | bytes 442376 | tf_op jit(solution)/shard_map/ppermute | solution.py:303
  116.9 8.7 %collective-permute-start.2 = (bf16[2,288,128]{2,1,0:T(8,128)(2,1)S(1)}, bf16[2,288,128]{2,1,0:T(8,128)(2,1)S(1)}, u32[]{:S(2)}, u32[]{:S(2)}) collective-permute-start(bf16[2,288,128]{2,1,0:T(8,128)(2,1)S(1)} %pad_maximum_fusion), channel_id=1, source_target_pairs={{0,1},{1,2},{2,3},{4,5},{5,6},{6,7},{8,9},{9,10},{10,11},{12,13},{... | collective-permute-start | bytes 442376 | tf_op jit(solution)/shard_map/ppermute | solution.py:302
  124.9 0.7 copy-start.7
  125.6 0.7 copy-start.8
  178.1 54.6 %all-to-all-start.1 = ((bf16[32,256,128]{2,1,0:T(8,128)(2,1)}), bf16[32,256,128]{2,1,0:T(8,128)(2,1)S(1)}, u32[]{:S(2)}, u32[]{:S(2)}) async-start(bf16[32,256,128]{2,1,0:T(8,128)(2,1)} %bitcast.48), calls=%async_computation.1 | async-start | bytes 4194304 | tf_op jit(solution)/shard_map/all_to_all | solution.py:242
  232.7 1.3 copy-start.1

commit v2 on v1

--- a/solution.py
+++ b/solution.py
@@ -19,9 +19,25 @@
     return pltpu.CompilerParams(vmem_limit_bytes=VMEM_BYTES)
 
 
+def turned(rows, d, capacity, kept):
+    at = pl.ds(pl.multiple_of(d * capacity, 16), capacity)
+    return rows[at, :].T[:kept].astype(jnp.bfloat16)
+
+
+def turn_back(rows, got_ref):
+    devices, kept, capacity = got_ref.shape
+
+    @pl.loop(0, devices)
+    def _(d):
+        block = got_ref[d].astype(jnp.float32)
+        block = jnp.concatenate([block, jnp.zeros((LANES - kept, capacity), jnp.float32)], axis=0)
+        rows[pl.ds(pl.multiple_of(d * capacity, 16), capacity), :] = block.T
+
+
 def route_kernel(features, columns, pos_ref, cell_ref, rec_ref, w_ref, off_ref, out_ref, emb, slots):
     rows = rec_ref.shape[0]
-    total = out_ref.shape[0]
+    devices, sent, capacity = out_ref.shape
+    total = devices * capacity
 
     @pl.loop(0, total // 128)
     def _(b):
@@ -46,20 +62,15 @@
             i = b * 16 + j
             slots[pl.ds(pos_ref[i], 1), :] = emb[pl.ds(i, 1), :]
 
-    @pl.loop(0, total // 128)
-    def _(b):
-        at = pl.ds(pl.multiple_of(b * 128, 128), 128)
-        out_ref[at, :] = slots[at, :].astype(jnp.bfloat16)
+    @pl.loop(0, devices)
+    def _(d):
+        out_ref[d] = turned(slots, d, capacity, sent)
 
 
 def merge_kernel(cell_ref, proj_ref, arr_ref, out_ref, rows32, s1, s2, s3, s0):
-    total = arr_ref.shape[0]
+    total = rows32.shape[0]
     cells = proj_ref.shape[0]
-
-    @pl.loop(0, total // 128)
-    def _(b):
-        at = pl.ds(pl.multiple_of(b * 128, 128), 128)
-        rows32[at, :] = arr_ref[at, :].astype(jnp.float32)
+    turn_back(rows32, arr_ref)
 
     @pl.loop(0, cells // 128)
     def _(b):
@@ -87,12 +98,52 @@
 
 
 def pair_dot(patches, row, width, w_ref):
-    y = None
-    for dr in range(4):
-        lhs = jnp.concatenate([patches[row + dr, k, pl.ds(0, width), :] for k in range(3)], axis=1)
-        part = jnp.dot(lhs, w_ref[pl.ds(dr * 384, 384), :], preferred_element_type=jnp.float32)
-        y = part if y is None else y + part
-    return y
+    lhs = jnp.concatenate(
+        [patches[row + dr, k, pl.ds(0, width), :] for dr in range(4) for k in range(3)], axis=1
+    )
+    return jnp.dot(lhs, w_ref[...], preferred_element_type=jnp.float32)
+
+
+def halo_kernel(
+    lon_size, lat_size, m_ref, left_ref, right_ref, top_ref, bottom_ref, send_sem, recv_sem
+):
+    height, width, _ = m_ref.shape
+    lon, lat = lax.axis_index("lon"), lax.axis_index("lat")
+    ways = [(a, b) for a in (-1, 0, 1) for b in (-1, 0, 1) if (a, b) != (0, 0)]
+
+    def there(a, b):
+        return (lax.rem(lon + a + lon_size, lon_size), lax.rem(lat + b + lat_size, lat_size))
+
+    barrier = pltpu.get_barrier_semaphore()
+    for a, b in ways:
+        pl.semaphore_signal(
+            barrier, inc=1, device_id=there(a, b), device_id_type=pl.DeviceIdType.MESH
+        )
+    pl.semaphore_wait(barrier, len(ways))
+
+    from_columns = {1: pl.ds(width - EDGE, EDGE), 0: pl.ds(0, width), -1: pl.ds(0, EDGE)}
+    to_columns = {1: pl.ds(0, EDGE), 0: pl.ds(EDGE, width), -1: pl.ds(EDGE + width, EDGE)}
+    from_rows = {1: pl.ds(height - 2, 2), 0: pl.ds(0, height), -1: pl.ds(0, 2)}
+    copies = []
+    for n, (a, b) in enumerate(ways):
+        if b == 0:
+            target = left_ref if a == 1 else right_ref
+        else:
+            target = (top_ref if b == 1 else bottom_ref).at[:, to_columns[a], :]
+        copies.append(
+            pltpu.make_async_remote_copy(
+                src_ref=m_ref.at[from_rows[b], from_columns[a], :],
+                dst_ref=target,
+                send_sem=send_sem.at[n],
+                recv_sem=recv_sem.at[n],
+                device_id=there(a, b),
+                device_id_type=pl.DeviceIdType.MESH,
+            )
+        )
+    for copy in copies:
+        copy.start()
+    for copy in copies:
+        copy.wait()
 
 
 def conv_kernel(
@@ -106,9 +157,9 @@
         for k in range(3):
             patches[row, k, :, :] = wide[pl.ds(EDGE - 2 + k, tall), :].astype(jnp.bfloat16)
 
-    for ref, base in ((top_ref, 0), (bottom_ref, height + 2)):
+    for n, ref, base in ((0, top_ref, 0), (1, bottom_ref, height + 2)):
         for t in range(2):
-            wide[...] = ref[t].astype(jnp.float32)
+            wide[...] = jnp.where(ends_ref[n] == 1, 0.0, ref[t].astype(jnp.float32))
             spread(base + t)
 
     @pl.loop(0, height)
@@ -139,28 +190,22 @@
             corr[pl.ds(pl.multiple_of(r * width, 128), width), :] = v
             out_ref[r] = v.T[:features].astype(jnp.bfloat16)
 
-    total = got_ref.shape[0]
-
-    @pl.loop(0, total // 16)
+    devices, kept, capacity = got_ref.shape
+
+    @pl.loop(0, devices * capacity // 16)
     def _(b):
         for j in range(16):
             i = b * 16 + j
             stage[pl.ds(i, 1), :] = corr[pl.ds(cell_ref[i], 1), :]
 
-    @pl.loop(0, total // 128)
-    def _(b):
-        at = pl.ds(pl.multiple_of(b * 128, 128), 128)
-        got_ref[at, :] = stage[at, :].astype(jnp.bfloat16)
+    @pl.loop(0, devices)
+    def _(d):
+        got_ref[d] = turned(stage, d, capacity, kept)
 
 
 def return_kernel(features, pos_ref, got_ref, out_ref, rows32, stage):
-    total = got_ref.shape[0]
-    rows = out_ref.shape[0]
-
-    @pl.loop(0, total // 128)
-    def _(b):
-        at = pl.ds(pl.multiple_of(b * 128, 128), 128)
-        rows32[at, :] = got_ref[at, :].astype(jnp.float32)
+    rows = out_ref.shape[1]
+    turn_back(rows32, got_ref)
 
     @pl.loop(0, rows // 16)
     def _(b):
@@ -171,7 +216,7 @@
     @pl.loop(0, rows // 128)
     def _(b):
         at = pl.ds(pl.multiple_of(b * 128, 128), 128)
-        out_ref[at, :] = stage[at, :][:, :features].astype(jnp.bfloat16)
+        out_ref[:, at] = stage[at, :].T[:features].astype(jnp.bfloat16)
 
 
 def slots_of(tile, devices, capacity):
@@ -240,17 +285,17 @@
 
     def exchange(rows):
         return lax.all_to_all(
-            rows.reshape(devices, capacity, LANES),
+            rows,
             ("lon", "lat"),
             split_axis=0,
             concat_axis=0,
             tiled=True,
-        ).reshape(slot_total, LANES)
+        )
 
     position = slots_of(gauge_block_number[:, 0], devices, capacity)
     payload = pl.pallas_call(
         functools.partial(route_kernel, features, width),
-        out_shape=jax.ShapeDtypeStruct((slot_total, LANES), bf16),
+        out_shape=jax.ShapeDtypeStruct((devices, features + 8, capacity), bf16),
         in_specs=[SMEM, VMEM, VMEM, VMEM, VMEM],
         out_specs=VMEM,
         scratch_shapes=[
@@ -267,8 +312,8 @@
         jnp.pad(gauge_scatter_offset, (0, more))[None],
     )
     arrived = exchange(payload)
-    line = arrived[:, features].astype(jnp.int32)
-    place = arrived[:, features + 1].astype(jnp.int32)
+    line = arrived[:, features].astype(jnp.int32).reshape(slot_total)
+    place = arrived[:, features + 1].astype(jnp.int32).reshape(slot_total)
     cell = jnp.clip((line - 1) * width + place, 0, cells - 1)
 
     projected = lax.dot_general(
@@ -289,18 +334,18 @@
         name="merge",
     )(cell, projected, arrived).reshape(height, width, LANES)
 
-    around = [(i, (i + 1) % lon_size) for i in range(lon_size)]
-    back = [(b, a) for a, b in around]
-    left = lax.ppermute(merged[:, width - EDGE:], "lon", around)
-    right = lax.ppermute(merged[:, :EDGE], "lon", back)
-    down = [(i, i + 1) for i in range(lat_size - 1)]
-    up = [(b, a) for a, b in down]
-
-    def strip(at):
-        return jnp.concatenate([left[at], merged[at], right[at]], axis=1)
-
-    top = lax.ppermute(strip(slice(height - 2, height)), "lat", down)
-    bottom = lax.ppermute(strip(slice(0, 2)), "lat", up)
+    side = jax.ShapeDtypeStruct((height, EDGE, LANES), bf16)
+    strip = jax.ShapeDtypeStruct((2, width + 2 * EDGE, LANES), bf16)
+    anywhere = pl.BlockSpec(memory_space=pl.ANY)
+    left, right, top, bottom = pl.pallas_call(
+        functools.partial(halo_kernel, lon_size, lat_size),
+        out_shape=(side, side, strip, strip),
+        in_specs=[anywhere],
+        out_specs=(anywhere,) * 4,
+        scratch_shapes=[pltpu.SemaphoreType.DMA((8,)), pltpu.SemaphoreType.DMA((8,))],
+        compiler_params=pltpu.CompilerParams(collective_id=0, has_side_effects=True),
+        name="halo",
+    )(merged)
     me = lax.axis_index("lat")
     ends = jnp.stack([(me == 0).astype(jnp.int32), (me == lat_size - 1).astype(jnp.int32)])
 
@@ -308,7 +353,7 @@
         functools.partial(conv_kernel, features),
         out_shape=(
             jax.ShapeDtypeStruct((height, features, width), bf16),
-            jax.ShapeDtypeStruct((slot_total, LANES), bf16),
+            jax.ShapeDtypeStruct((devices, features, capacity), bf16),
         ),
         in_specs=[SMEM, SMEM] + [VMEM] * 9,
         out_specs=(VMEM, VMEM),
@@ -336,7 +381,7 @@
 
     station_values = pl.pallas_call(
         functools.partial(return_kernel, features),
-        out_shape=jax.ShapeDtypeStruct((held_rows, features), bf16),
+        out_shape=jax.ShapeDtypeStruct((features, held_rows), bf16),
         in_specs=[SMEM, VMEM],
         out_specs=VMEM,
         scratch_shapes=[
@@ -346,7 +391,7 @@
         compiler_params=params(),
         name="unroute",
     )(position, exchange(picked))
-    return (jnp.transpose(corrected, (1, 0, 2)), station_values)
+    return (jnp.transpose(corrected, (1, 0, 2)), station_values.T)
 
 
 def solution(mesh):

time: 245 us -> 218 us (0.89)
  waiting for transfers between devices: 66.2 us -> 38.4 us
  Pallas kernels: 96.9 us -> 120 us
  starting transfers between devices: 23.5 us -> 10.3 us
  local copies, waits for them, and re-layouts: 31.8 us -> 26.7 us
  other arithmetic: 9.13 us -> 5.49 us
    all_to_all x2, waiting for transfers between devices: 61.1 us -> 38.4 us  [exchange(): lax.all_to_all(rows, ('lon', 'lat'), split_axis=0, concat_axis=0, tiled=T...]
    pallas_call x0 -> x1, Pallas kernels: none -> 11.7 us  [on_device(): pl.pallas_call(functools.partial(halo_kernel, lon_size, lat_size), out_sh...]
    ppermute x4 -> x0, starting transfers between devices: 10.3 us -> none  [the longest x1 4.55 us: on_device(): top = lax.ppermute(strip(slice(height - 2, height)), 'lat', down)]
    pallas_call x1, Pallas kernels: 23.7 us -> 29.8 us  [on_device(): pl.pallas_call(merge_kernel, out_shape=jax.ShapeDtypeStruct((cells, LANES...]
    pallas_call x1, Pallas kernels: 7.87 us -> 13 us  [on_device(): pl.pallas_call(functools.partial(return_kernel, features), out_shape=jax....]
    ppermute x4 -> x0, waiting for transfers between devices: 5.11 us -> none  [the longest x1 2.88 us: on_device(): left = lax.ppermute(merged[:, width - EDGE:], 'lon', around)]
    unnamed x30 -> x19, local copies, waits for them, and re-layouts: 25.4 us -> 22.4 us
    all_to_all x2, starting transfers between devices: 13.2 us -> 10.3 us  [exchange(): lax.all_to_all(rows, ('lon', 'lat'), split_axis=0, concat_axis=0, tiled=T...]
  transfers between devices with their start and end apart: 6 -> 2, of which waited for: 5 -> 2; matrix products, arithmetic and copies ran while one was open for 17% -> 18% of each run, Pallas kernels for 0% -> 0%
where the time goes in v2:
time: 218 us; the launch traced here: 217 us
  Pallas kernels  120 us (55%)
  waiting for transfers between devices  38.4 us (18%)
  local copies, waits for them, and re-layouts  26.7 us (12%)
  matrix products  15.8 us (7%)
  starting transfers between devices  10.3 us (5%)
  other arithmetic  5.49 us (3%)
    pallas_call x1, Pallas kernels, on_device(): pl.pallas_call(functools.partial(conv_kernel, features), out_shape=(jax.S...  49.2 us
    all_to_all x2, waiting for transfers between devices, exchange(): lax.all_to_all(rows, ('lon', 'lat'), split_axis=0, concat_axis=0, tiled=T...  38.4 us
    pallas_call x1, Pallas kernels, on_device(): pl.pallas_call(merge_kernel, out_shape=jax.ShapeDtypeStruct((cells, LANES...  29.8 us
    unnamed x19, local copies, waits for them, and re-layouts  22.4 us
    pallas_call x1, Pallas kernels, on_device(): pl.pallas_call(functools.partial(route_kernel, features, width), out_shap...  16 us
    dot_general x1, matrix products, on_device(): lax.dot_general(ensemble_prediction.reshape(depth, cells), jnp.pad(mappin...  14.6 us
    pallas_call x1, Pallas kernels, on_device(): pl.pallas_call(functools.partial(return_kernel, features), out_shape=jax....  13 us
    pallas_call x1, Pallas kernels, on_device(): pl.pallas_call(functools.partial(halo_kernel, lon_size, lat_size), out_sh...  11.7 us
  transfers between devices with their start and end apart: 2, of which 2 were waited for; matrix products, arithmetic and copies ran while one was open for 18% of the time, Pallas kernels for 0%

profile of v2, /device:TPU:0, one launch (start us, length us, event | category | flops | bytes accessed | tf_op | source)
XLA Modules:
  0.0 217.0 jit_solution(17169072031209577401)
XLA Ops:
  0.7 0.7 broadcast_multiply_fusion
  1.4 0.9 convert_reduce_fusion
  2.3 0.9 copy.24
  3.2 1.2 pad_bitcast_fusion.off_ref
  4.4 0.2 select_reduce_fusion
  4.6 1.1 fusion.7
  5.8 0.6 bitcast_add_fusion.pos_ref
  6.4 0.6 pad.42.w_ref
  7.0 16.0 %route.1 = bf16[32,104,256]{2,1,0:T(8,128)(2,1)} custom-call(s32[4096]{0:T(1024)} %bitcast_add_fusion.pos_ref, s32[32,128]{1,0:T(8,128)} %bitcast.48, bf16[4096,256]{1,0:T(8,128)(2,1)} %rec_ref.1, bf16[256,128]{1,0:T(8,128)(2,1)} %pad.42.w_ref, f32[1,128]{1,0:T(1,128)} %pad_bitcast_fusion.off_ref), custom_call_target="tpu_custom_call" | custom-call | tf_op jit(solution)/shard_map/route/pallas_call | solution.py:296
  23.0 7.3 %all-to-all-start = ((bf16[32,104,256]{2,1,0:T(8,128)(2,1)}), bf16[32,104,256]{2,1,0:T(8,128)(2,1)S(1)}, u32[]{:S(2)}, u32[]{:S(2)}) async-start(bf16[32,104,256]{2,1,0:T(8,128)(2,1)} %route.1), calls=%async_computation | async-start | bytes 3407872 | tf_op jit(solution)/shard_map/all_to_all | solution.py:287
  30.3 0.0 copy-start.2
  30.3 14.7 %copy.32 = bf16[51,8,64,256]{3,1,2,0:T(8,128)(2,1)} copy(bf16[51,8,64,256]{3,2,1,0:T(8,128)(2,1)} %bitcast.36) | data formatting | bytes 26738688
  45.0 0.0 copy-start.3
  45.0 0.0 copy-done.2
  45.0 0.1 pad.46
  45.1 0.1 fusion.8
  45.2 1.2 copy.27
  46.4 0.0 copy-start.5
  46.4 0.0 copy-start.6
  46.4 0.0 copy-start.7
  46.4 0.0 copy-start.4
  46.4 0.0 copy-done.3
  46.4 0.1 pad.50
  46.5 0.1 fusion.9
  46.6 1.2 copy.28
  47.8 0.0 copy-done.5
  47.8 0.0 copy-done.6
  47.8 0.0 copy-done.7
  47.8 0.7 add_convert_fusion.ends_ref
  48.5 0.6 pad_maximum_fusion
  49.1 0.6 pad_maximum_fusion.1
  49.7 0.0 copy-done.4
  49.7 14.6 %fusion.proj_ref = f32[16384,128]{1,0:T(8,128)} fusion(bf16[408,16384]{1,0:T(8,128)(2,1)} %bitcast.33, f32[128]{0:T(128)S(1)} %pad.45, bf16[96,408]{1,0:T(8,128)(2,1)S(1)} %copy-done.4), kind=kOutput, calls=%fused_computation.1 | convolution fusion | flops 1713373184 | bytes 21836800 | tf_op jit(solution)/shard_map/dot_general | solution.py:319
  64.3 6.3 %all-to-all-done.arr_ref = bf16[32,104,256]{2,1,0:T(8,128)(2,1)S(1)} async-done(((bf16[32,104,256]{2,1,0:T(8,128)(2,1)}), bf16[32,104,256]{2,1,0:T(8,128)(2,1)S(1)}, u32[]{:S(2)}, u32[]{:S(2)}) %all-to-all-start) | async-done | bytes 1703968 | tf_op jit(solution)/shard_map/all_to_all | solution.py:287
  70.6 0.0 copy-start
  70.6 0.9 fusion.17
  71.5 0.3 copy-done
  71.8 29.8 %merge.1 = bf16[16384,128]{1,0:T(8,128)(2,1)} custom-call(s32[8192]{0:T(1024)} %bitcast.41, f32[16384,128]{1,0:T(8,128)} %fusion.proj_ref, bf16[32,104,256]{2,1,0:T(8,128)(2,1)} %copy-done), custom_call_target="tpu_custom_call" | custom-call | tf_op jit(solution)/shard_map/merge/pallas_call | solution.py:327
  101.6 11.7 %halo.1 = (bf16[64,16,128]{2,1,0:T(8,128)(2,1)}, bf16[64,16,128]{2,1,0:T(8,128)(2,1)}, bf16[2,288,128]{2,1,0:T(8,128)(2,1)}, bf16[2,288,128]{2,1,0:T(8,128)(2,1)}) custom-call(bf16[64,256,128]{2,1,0:T(8,128)(2,1)} %bitcast.34), custom_call_target="tpu_custom_call" | custom-call | tf_op jit(solution)/shard_map/halo/pallas_call | solution.py:340
  113.2 49.2 %convs.1 = (bf16[64,96,256]{2,1,0:T(8,128)(2,1)}, bf16[32,96,256]{2,1,0:T(8,128)(2,1)}) custom-call(s32[2]{0:T(128)} %add_convert_fusion.ends_ref, s32[8192]{0:T(1024)} %bitcast.42, bf16[64,256,128]{2,1,0:T(8,128)(2,1)} %bitcast.35, bf16[64,16,128]{2,1,0:T(8,128)(2,1)} %get-tuple-element.8.left_ref, bf16[64,16,128]{2,1,0:T(8,128)(2,1)} %get-tuple-element.9.right_ref, ...), custom_call_target="tpu_custom_call" | custom-call | tf_op jit(solution)/shard_map/convs/pallas_call | solution.py:352
  162.4 3.0 %all-to-all-start.1 = ((bf16[32,96,256]{2,1,0:T(8,128)(2,1)}), bf16[32,96,256]{2,1,0:T(8,128)(2,1)S(1)}, u32[]{:S(2)}, u32[]{:S(2)}) async-start(bf16[32,96,256]{2,1,0:T(8,128)(2,1)} %get-tuple-element.13), calls=%async_computation.1 | async-start | bytes 3145728 | tf_op jit(solution)/shard_map/all_to_all | solution.py:287
  165.4 5.3 %copy.29 = bf16[96,64,256]{2,1,0:T(8,128)(2,1)} copy(bf16[96,64,256]{2,0,1:T(8,128)(2,1)} %bitcast.39) | data formatting | bytes 6291456
  170.7 32.1 %all-to-all-done.1.got_ref = bf16[32,96,256]{2,1,0:T(8,128)(2,1)S(1)} async-done(((bf16[32,96,256]{2,1,0:T(8,128)(2,1)}), bf16[32,96,256]{2,1,0:T(8,128)(2,1)S(1)}, u32[]{:S(2)}, u32[]{:S(2)}) %all-to-all-start.1) | async-done | bytes 1572896 | tf_op jit(solution)/shard_map/all_to_all | solution.py:287
  202.9 0.0 copy-start.1
  202.9 1.2 copy-done.1
  204.0 13.0 %unroute.1 = bf16[96,4096]{1,0:T(8,128)(2,1)} custom-call(s32[4096]{0:T(1024)} %bitcast_add_fusion.pos_ref, bf16[32,96,256]{2,1,0:T(8,128)(2,1)} %copy-done.1), custom_call_target="tpu_custom_call" | custom-call | tf_op jit(solution)/shard_map/unroute/pallas_call | solution.py:382
  (5 shorter events, 0.0 us)
Async XLA Ops:
  23.0 47.6 %all-to-all-start = ((bf16[32,104,256]{2,1,0:T(8,128)(2,1)}), bf16[32,104,256]{2,1,0:T(8,128)(2,1)S(1)}, u32[]{:S(2)}, u32[]{:S(2)}) async-start(bf16[32,104,256]{2,1,0:T(8,128)(2,1)} %route.1), calls=%async_computation | async-start | bytes 3407872 | tf_op jit(solution)/shard_map/all_to_all | solution.py:287
  30.3 14.7 %copy-start.2 = (bf16[96,96,3,3]{1,0,3,2:T(8,128)(2,1)S(1)}, bf16[96,96,3,3]{1,0,3,2:T(8,128)(2,1)}, u32[]{:S(2)}) copy-start(bf16[96,96,3,3]{1,0,3,2:T(8,128)(2,1)} %param.20) | copy-start | bytes 497668
  45.0 1.4 copy-start.3
  46.4 1.4 copy-start.5
  46.4 1.4 copy-start.6
  46.4 1.4 copy-start.7
  46.4 3.3 %copy-start.4 = (bf16[96,408]{1,0:T(8,128)(2,1)S(1)}, bf16[96,408]{1,0:T(8,128)(2,1)}, u32[]{:S(2)}) copy-start(bf16[96,408]{1,0:T(8,128)(2,1)} %param.13) | copy-start | bytes 235012
  70.6 1.2 copy-start
  162.4 40.5 %all-to-all-start.1 = ((bf16[32,96,256]{2,1,0:T(8,128)(2,1)}), bf16[32,96,256]{2,1,0:T(8,128)(2,1)S(1)}, u32[]{:S(2)}, u32[]{:S(2)}) async-start(bf16[32,96,256]{2,1,0:T(8,128)(2,1)} %get-tuple-element.13), calls=%async_computation.1 | async-start | bytes 3145728 | tf_op jit(solution)/shard_map/all_to_all | solution.py:287
  202.9 1.2 copy-start.1

commit v3 on v2

--- a/solution.py
+++ b/solution.py
@@ -27,7 +27,7 @@
 def turn_back(rows, got_ref):
     devices, kept, capacity = got_ref.shape
 
-    @pl.loop(0, devices)
+    @pl.loop(0, devices, unroll=4)
     def _(d):
         block = got_ref[d].astype(jnp.float32)
         block = jnp.concatenate([block, jnp.zeros((LANES - kept, capacity), jnp.float32)], axis=0)
@@ -39,13 +39,13 @@
     devices, sent, capacity = out_ref.shape
     total = devices * capacity
 
-    @pl.loop(0, total // 128)
+    @pl.loop(0, total // 128, unroll=4)
     def _(b):
         slots[pl.ds(pl.multiple_of(b * 128, 128), 128), :] = jnp.zeros((128, LANES), jnp.float32)
 
     lane = lax.broadcasted_iota(jnp.int32, (128, LANES), 1)
 
-    @pl.loop(0, rows // 128)
+    @pl.loop(0, rows // 128, unroll=4)
     def _(b):
         at = pl.ds(pl.multiple_of(b * 128, 128), 128)
         e = jnp.dot(rec_ref[at, :], w_ref[...], preferred_element_type=jnp.float32) + off_ref[...]
@@ -62,7 +62,7 @@
             i = b * 16 + j
             slots[pl.ds(pos_ref[i], 1), :] = emb[pl.ds(i, 1), :]
 
-    @pl.loop(0, devices)
+    @pl.loop(0, devices, unroll=4)
     def _(d):
         out_ref[d] = turned(slots, d, capacity, sent)
 
@@ -72,7 +72,7 @@
     cells = proj_ref.shape[0]
     turn_back(rows32, arr_ref)
 
-    @pl.loop(0, cells // 128)
+    @pl.loop(0, cells // 128, unroll=4)
     def _(b):
         at = pl.ds(pl.multiple_of(b * 128, 128), 128)
         for s in (s0, s1, s2, s3):
@@ -89,7 +89,7 @@
             for j in range(4):
                 sums[j][at[j], :] = new[j]
 
-    @pl.loop(0, cells // 128)
+    @pl.loop(0, cells // 128, unroll=4)
     def _(b):
         at = pl.ds(pl.multiple_of(b * 128, 128), 128)
         out_ref[at, :] = (
@@ -162,14 +162,14 @@
             wide[...] = jnp.where(ends_ref[n] == 1, 0.0, ref[t].astype(jnp.float32))
             spread(base + t)
 
-    @pl.loop(0, height)
+    @pl.loop(0, height, unroll=2)
     def _(r):
         wide[pl.ds(0, EDGE), :] = left_ref[r].astype(jnp.float32)
         wide[pl.ds(EDGE, width), :] = m_ref[r].astype(jnp.float32)
         wide[pl.ds(EDGE + width, EDGE), :] = right_ref[r].astype(jnp.float32)
         spread(r + 2)
 
-    @pl.loop(0, height // 2 + 1)
+    @pl.loop(0, height // 2 + 1, unroll=3)
     def _(p):
         y = pair_dot(patches, 2 * p, tall, w1_ref) + b1_ref[...]
         hidden = jax.nn.gelu(y)
@@ -181,7 +181,7 @@
             for k in range(3):
                 patches[h, k, pl.ds(0, width), :] = wide[pl.ds(k, width), :].astype(jnp.bfloat16)
 
-    @pl.loop(0, height // 2)
+    @pl.loop(0, height // 2, unroll=2)
     def _(p):
         y = pair_dot(patches, 2 * p, width, w2_ref) + b2_ref[...]
         for t in range(2):
@@ -198,7 +198,7 @@
             i = b * 16 + j
             stage[pl.ds(i, 1), :] = corr[pl.ds(cell_ref[i], 1), :]
 
-    @pl.loop(0, devices)
+    @pl.loop(0, devices, unroll=4)
     def _(d):
         got_ref[d] = turned(stage, d, capacity, kept)
 
@@ -213,7 +213,7 @@
             i = b * 16 + j
             stage[pl.ds(i, 1), :] = rows32[pl.ds(pos_ref[i], 1), :]
 
-    @pl.loop(0, rows // 128)
+    @pl.loop(0, rows // 128, unroll=4)
     def _(b):
         at = pl.ds(pl.multiple_of(b * 128, 128), 128)
         out_ref[:, at] = stage[at, :].T[:features].astype(jnp.bfloat16)

time: 218 us -> 197 us (0.904)
  Pallas kernels: 120 us -> 98.7 us
    pallas_call x1, Pallas kernels: 49.2 us -> 39.9 us  [on_device(): pl.pallas_call(functools.partial(conv_kernel, features), out_shape=(jax.S...]
    pallas_call x1, Pallas kernels: 29.8 us -> 24.8 us  [on_device(): pl.pallas_call(merge_kernel, out_shape=jax.ShapeDtypeStruct((cells, LANES...]
    pallas_call x1, Pallas kernels: 16 us -> 11.5 us  [on_device(): pl.pallas_call(functools.partial(route_kernel, features, width), out_shap...]
    pallas_call x1, Pallas kernels: 13 us -> 8.71 us  [on_device(): pl.pallas_call(functools.partial(return_kernel, features), out_shape=jax....]
    pallas_call x1, Pallas kernels: 11.7 us -> 13.9 us  [on_device(): pl.pallas_call(functools.partial(halo_kernel, lon_size, lat_size), out_sh...]
  transfers between devices with their start and end apart: 2 -> 2, of which waited for: 2 -> 2; matrix products, arithmetic and copies ran while one was open for 18% -> 20% of each run, Pallas kernels for 0% -> 0%
where the time goes in v3:
time: 197 us; the launch traced here: 196 us
  Pallas kernels  98.7 us (50%)
  waiting for transfers between devices  38.4 us (19%)
  local copies, waits for them, and re-layouts  26.7 us (14%)
  matrix products  15.8 us (8%)
  starting transfers between devices  9.98 us (5%)
  other arithmetic  5.49 us (3%)
    pallas_call x1, Pallas kernels, on_device(): pl.pallas_call(functools.partial(conv_kernel, features), out_shape=(jax.S...  39.9 us
    all_to_all x2, waiting for transfers between devices, exchange(): lax.all_to_all(rows, ('lon', 'lat'), split_axis=0, concat_axis=0, tiled=T...  38.4 us
    pallas_call x1, Pallas kernels, on_device(): pl.pallas_call(merge_kernel, out_shape=jax.ShapeDtypeStruct((cells, LANES...  24.8 us
    unnamed x19, local copies, waits for them, and re-layouts  22.4 us
    dot_general x1, matrix products, on_device(): lax.dot_general(ensemble_prediction.reshape(depth, cells), jnp.pad(mappin...  14.6 us
    pallas_call x1, Pallas kernels, on_device(): pl.pallas_call(functools.partial(halo_kernel, lon_size, lat_size), out_sh...  13.9 us
    pallas_call x1, Pallas kernels, on_device(): pl.pallas_call(functools.partial(route_kernel, features, width), out_shap...  11.5 us
    all_to_all x2, starting transfers between devices, exchange(): lax.all_to_all(rows, ('lon', 'lat'), split_axis=0, concat_axis=0, tiled=T...  9.98 us
  transfers between devices with their start and end apart: 2, of which 2 were waited for; matrix products, arithmetic and copies ran while one was open for 20% of the time, Pallas kernels for 0%

profile of v3, /device:TPU:0, one launch (start us, length us, event | category | flops | bytes accessed | tf_op | source)
XLA Modules:
  0.0 195.8 jit_solution(71363889408497679)
XLA Ops:
  0.7 0.7 broadcast_multiply_fusion
  1.4 0.9 convert_reduce_fusion
  2.3 0.9 copy.24
  3.2 1.2 pad_bitcast_fusion.off_ref
  4.4 0.2 select_reduce_fusion
  4.6 1.1 fusion.7
  5.8 0.6 bitcast_add_fusion.pos_ref
  6.4 0.6 pad.42.w_ref
  7.0 11.5 %route.1 = bf16[32,104,256]{2,1,0:T(8,128)(2,1)} custom-call(s32[4096]{0:T(1024)} %bitcast_add_fusion.pos_ref, s32[32,128]{1,0:T(8,128)} %bitcast.48, bf16[4096,256]{1,0:T(8,128)(2,1)} %rec_ref.1, bf16[256,128]{1,0:T(8,128)(2,1)} %pad.42.w_ref, f32[1,128]{1,0:T(1,128)} %pad_bitcast_fusion.off_ref), custom_call_target="tpu_custom_call" | custom-call | tf_op jit(solution)/shard_map/route/pallas_call | solution.py:296
  18.5 7.3 %all-to-all-start = ((bf16[32,104,256]{2,1,0:T(8,128)(2,1)}), bf16[32,104,256]{2,1,0:T(8,128)(2,1)S(1)}, u32[]{:S(2)}, u32[]{:S(2)}) async-start(bf16[32,104,256]{2,1,0:T(8,128)(2,1)} %route.1), calls=%async_computation | async-start | bytes 3407872 | tf_op jit(solution)/shard_map/all_to_all | solution.py:287
  25.8 0.0 copy-start.2
  25.8 14.7 %copy.32 = bf16[51,8,64,256]{3,1,2,0:T(8,128)(2,1)} copy(bf16[51,8,64,256]{3,2,1,0:T(8,128)(2,1)} %bitcast.36) | data formatting | bytes 26738688
  40.5 0.0 copy-start.3
  40.5 0.0 copy-done.2
  40.5 0.1 pad.46
  40.6 0.1 fusion.8
  40.7 1.2 copy.27
  41.9 0.0 copy-start.5
  41.9 0.0 copy-start.6
  41.9 0.0 copy-start.7
  41.9 0.0 copy-start.4
  41.9 0.0 copy-done.3
  41.9 0.1 pad.50
  42.0 0.1 fusion.9
  42.1 1.2 copy.28
  43.3 0.0 copy-done.5
  43.3 0.0 copy-done.6
  43.3 0.0 copy-done.7
  43.4 0.7 add_convert_fusion.ends_ref
  44.0 0.6 pad_maximum_fusion
  44.6 0.6 pad_maximum_fusion.1
  45.2 0.0 copy-done.4
  45.2 14.6 %fusion.proj_ref = f32[16384,128]{1,0:T(8,128)} fusion(bf16[408,16384]{1,0:T(8,128)(2,1)} %bitcast.33, f32[128]{0:T(128)S(1)} %pad.45, bf16[96,408]{1,0:T(8,128)(2,1)S(1)} %copy-done.4), kind=kOutput, calls=%fused_computation.1 | convolution fusion | flops 1713373184 | bytes 21836800 | tf_op jit(solution)/shard_map/dot_general | solution.py:319
  59.8 6.3 %all-to-all-done.arr_ref = bf16[32,104,256]{2,1,0:T(8,128)(2,1)S(1)} async-done(((bf16[32,104,256]{2,1,0:T(8,128)(2,1)}), bf16[32,104,256]{2,1,0:T(8,128)(2,1)S(1)}, u32[]{:S(2)}, u32[]{:S(2)}) %all-to-all-start) | async-done | bytes 1703968 | tf_op jit(solution)/shard_map/all_to_all | solution.py:287
  66.1 0.0 copy-start
  66.1 0.9 fusion.17
  67.0 0.3 copy-done
  67.3 24.8 %merge.1 = bf16[16384,128]{1,0:T(8,128)(2,1)} custom-call(s32[8192]{0:T(1024)} %bitcast.41, f32[16384,128]{1,0:T(8,128)} %fusion.proj_ref, bf16[32,104,256]{2,1,0:T(8,128)(2,1)} %copy-done), custom_call_target="tpu_custom_call" | custom-call | tf_op jit(solution)/shard_map/merge/pallas_call | solution.py:327
  92.1 13.9 %halo.1 = (bf16[64,16,128]{2,1,0:T(8,128)(2,1)}, bf16[64,16,128]{2,1,0:T(8,128)(2,1)}, bf16[2,288,128]{2,1,0:T(8,128)(2,1)}, bf16[2,288,128]{2,1,0:T(8,128)(2,1)}) custom-call(bf16[64,256,128]{2,1,0:T(8,128)(2,1)} %bitcast.34), custom_call_target="tpu_custom_call" | custom-call | tf_op jit(solution)/shard_map/halo/pallas_call | solution.py:340
  105.9 39.9 %convs.1 = (bf16[64,96,256]{2,1,0:T(8,128)(2,1)}, bf16[32,96,256]{2,1,0:T(8,128)(2,1)}) custom-call(s32[2]{0:T(128)} %add_convert_fusion.ends_ref, s32[8192]{0:T(1024)} %bitcast.42, bf16[64,256,128]{2,1,0:T(8,128)(2,1)} %bitcast.35, bf16[64,16,128]{2,1,0:T(8,128)(2,1)} %get-tuple-element.8.left_ref, bf16[64,16,128]{2,1,0:T(8,128)(2,1)} %get-tuple-element.9.right_ref, ...), custom_call_target="tpu_custom_call" | custom-call | tf_op jit(solution)/shard_map/convs/pallas_call | solution.py:352
  145.8 2.7 %all-to-all-start.1 = ((bf16[32,96,256]{2,1,0:T(8,128)(2,1)}), bf16[32,96,256]{2,1,0:T(8,128)(2,1)S(1)}, u32[]{:S(2)}, u32[]{:S(2)}) async-start(bf16[32,96,256]{2,1,0:T(8,128)(2,1)} %get-tuple-element.13), calls=%async_computation.1 | async-start | bytes 3145728 | tf_op jit(solution)/shard_map/all_to_all | solution.py:287
  148.5 5.3 %copy.29 = bf16[96,64,256]{2,1,0:T(8,128)(2,1)} copy(bf16[96,64,256]{2,0,1:T(8,128)(2,1)} %bitcast.39) | data formatting | bytes 6291456
  153.8 32.1 %all-to-all-done.1.got_ref = bf16[32,96,256]{2,1,0:T(8,128)(2,1)S(1)} async-done(((bf16[32,96,256]{2,1,0:T(8,128)(2,1)}), bf16[32,96,256]{2,1,0:T(8,128)(2,1)S(1)}, u32[]{:S(2)}, u32[]{:S(2)}) %all-to-all-start.1) | async-done | bytes 1572896 | tf_op jit(solution)/shard_map/all_to_all | solution.py:287
  186.0 0.0 copy-start.1
  186.0 1.2 copy-done.1
  187.1 8.7 %unroute.1 = bf16[96,4096]{1,0:T(8,128)(2,1)} custom-call(s32[4096]{0:T(1024)} %bitcast_add_fusion.pos_ref, bf16[32,96,256]{2,1,0:T(8,128)(2,1)} %copy-done.1), custom_call_target="tpu_custom_call" | custom-call | tf_op jit(solution)/shard_map/unroute/pallas_call | solution.py:382
  (5 shorter events, 0.0 us)
Async XLA Ops:
  18.5 47.6 %all-to-all-start = ((bf16[32,104,256]{2,1,0:T(8,128)(2,1)}), bf16[32,104,256]{2,1,0:T(8,128)(2,1)S(1)}, u32[]{:S(2)}, u32[]{:S(2)}) async-start(bf16[32,104,256]{2,1,0:T(8,128)(2,1)} %route.1), calls=%async_computation | async-start | bytes 3407872 | tf_op jit(solution)/shard_map/all_to_all | solution.py:287
  25.8 14.7 %copy-start.2 = (bf16[96,96,3,3]{1,0,3,2:T(8,128)(2,1)S(1)}, bf16[96,96,3,3]{1,0,3,2:T(8,128)(2,1)}, u32[]{:S(2)}) copy-start(bf16[96,96,3,3]{1,0,3,2:T(8,128)(2,1)} %param.20) | copy-start | bytes 497668
  40.5 1.4 copy-start.3
  41.9 1.4 copy-start.5
  41.9 1.4 copy-start.6
  41.9 1.4 copy-start.7
  41.9 3.3 %copy-start.4 = (bf16[96,408]{1,0:T(8,128)(2,1)S(1)}, bf16[96,408]{1,0:T(8,128)(2,1)}, u32[]{:S(2)}) copy-start(bf16[96,408]{1,0:T(8,128)(2,1)} %param.13) | copy-start | bytes 235012
  66.1 1.2 copy-start
  145.8 40.1 %all-to-all-start.1 = ((bf16[32,96,256]{2,1,0:T(8,128)(2,1)}), bf16[32,96,256]{2,1,0:T(8,128)(2,1)S(1)}, u32[]{:S(2)}, u32[]{:S(2)}) async-start(bf16[32,96,256]{2,1,0:T(8,128)(2,1)} %get-tuple-element.13), calls=%async_computation.1 | async-start | bytes 3145728 | tf_op jit(solution)/shard_map/all_to_all | solution.py:287
  186.0 1.2 copy-start.1
